TPU v7x, 512 devices: a whole 4x8x8 slice. The times are simulated.
512 devices in a mesh: req: 64 (over z, x, core), tensor: 8 (over y).
Axes of the slice: x: 4, y: 8, z: 8, core: 2. Of those that a mesh axis runs over, the one named last changes fastest.
Arguments:
- prompts: bfloat16 [32768, 4096], P(('req', 'tensor')), may hold values from -6 to 6
- layer_norm_gain: float32 [4096], replicated, may hold values from 0.1 to 1.9
- query_base_matrix: bfloat16 [4096, 4096], P('req', 'tensor'), may hold values from -0.09375 to 0.09375
- adapter_down_weight: bfloat16 [128, 32, 4096], P('req', None, 'tensor'), may hold values from -0.09375 to 0.09375
- adapter_up_weight: bfloat16 [128, 32, 4096], P('req', None, 'tensor'), may hold values from -1 to 1
- request_prompt_length: int32 [64], P('req'), may hold values from 128 to 512, as said below
- request_adapter_ident: int32 [64], P('req'), may hold values from 0 to 127
- adapter_pool_row: int32 [128], replicated, may hold values from 0 to 127, each once
Outputs:
- queries: bfloat16 [32768, 4096], P('req', 'tensor')
Inputs may be any that keep to these rules, and one draw needn't show every extreme that they name: `request_prompt_length`: lengths lie between 128 and 512; some request has exactly 512.
All inputs are finite; a program needn't handle non-finite values.
Results may differ from a plain program's by a relative error of at most 0.0054.
Values may be sent and summed in bfloat16 or wider, within the bound.
No kernel may reach another device: no remote copies, remote signals or barrier semaphores. Data moves between devices by JAX's collectives and lax.ppermute only.
A program may use at most 64 MiB of HBM per device.

v0:
```python
import jax
import jax.numpy as jnp
from jax import lax
from jax.sharding import PartitionSpec as P


def normalize(rows, layer_norm_gain):
    values = rows.astype(jnp.float32)
    scale = lax.rsqrt(jnp.mean(values * values, axis=-1, keepdims=True) + 1e-06)
    return (values * scale * layer_norm_gain).astype(jnp.bfloat16)


def per_device(
    prompts,
    layer_norm_gain,
    query_base_matrix,
    adapter_down_weight,
    adapter_up_weight,
    request_prompt_length,
    request_adapter_ident,
    adapter_pool_row,
):
    req_here = request_adapter_ident.shape[0]
    width = query_base_matrix.shape[1]
    whole = lax.all_gather(prompts, "tensor", axis=0, tiled=True)
    normed = normalize(whole, layer_norm_gain)
    row_count = normed.shape[0]
    span = row_count // req_here
    base = jnp.dot(
        normed,
        lax.all_gather(query_base_matrix, "req", axis=0, tiled=True),
        preferred_element_type=jnp.float32,
    )
    pool_total = adapter_pool_row.shape[0]
    hits = request_adapter_ident[:, None] == jnp.arange(pool_total, dtype=jnp.int32)[None, :]
    slots = jnp.sum(jnp.where(hits, adapter_pool_row[None, :], 0), axis=1)
    pieces = (
        lax.all_gather(adapter_down_weight, "req", axis=0, tiled=True),
        lax.all_gather(adapter_up_weight, "req", axis=0, tiled=True),
    )
    index = jnp.arange(pieces[0].shape[0], dtype=jnp.int32)
    onehot = (slots[:, None] == index[None, :]).astype(jnp.bfloat16)
    down_add = jnp.einsum("qk,kcd->qcd", onehot, pieces[0], preferred_element_type=jnp.float32)
    up_add = jnp.einsum("qk,kcd->qcd", onehot, pieces[1], preferred_element_type=jnp.float32)
    down_sel = down_add
    up_sel = up_add
    down_sel = down_sel.astype(jnp.bfloat16)
    up_sel = up_sel.astype(jnp.bfloat16)
    first_col = lax.axis_index("tensor") * width
    own_cols = lax.dynamic_slice_in_dim(normed, first_col, width, 1).reshape(req_here, span, width)
    partial_value = jnp.einsum(
        "qld,qcd->qlc", own_cols, down_sel, preferred_element_type=jnp.float32
    )
    low = lax.psum(partial_value, "tensor").astype(jnp.bfloat16)
    adapted = jnp.einsum("qlc,qcd->qld", low, up_sel, preferred_element_type=jnp.float32)
    total = base.reshape(req_here, span, width) + adapted
    valid = jnp.arange(span, dtype=jnp.int32)[None, :] < request_prompt_length[:, None]
    result = jnp.where(valid[:, :, None], total, 0.0)
    return result.reshape(row_count, width).astype(jnp.bfloat16)


def solution(mesh):
    in_specs = (
        P(("req", "tensor"), None),
        P(),
        P("req", "tensor"),
        P("req", None, "tensor"),
        P("req", None, "tensor"),
        P("req"),
        P("req"),
        P(),
    )
    out_specs = P("req", "tensor")
    return jax.shard_map(
        per_device, mesh=mesh, in_specs=in_specs, out_specs=out_specs, check_vma=False
    )
```

profile of v0, /device:TPU:1, one launch (start us, length us, event | category | flops | bytes accessed | tf_op | source)
XLA Modules:
  0.0 345.5 jit_solution(292919929853455260)
XLA Ops:
  6.5 0.0 copy-start.1
  6.5 0.0 all-gather.5.cloned.1.call-start
  6.5 0.7 all-gather.5.cloned.1.call-update
  7.3 0.0 all-gather.9.cloned.1.call-start
  7.3 0.7 all-gather.9.cloned.1.call-update
  8.0 0.0 all-gather.7.cloned.1.call-start
  8.1 0.7 all-gather.7.cloned.1.call-update
  8.7 0.0 all-gather.11.cloned.1.call-start
  8.8 0.5 all-gather.11.cloned.1.call-update
  10.6 1.3 fusion.18
  11.9 60.2 %all-gather.5.cloned.1.call-done = bf16[512,4096]{1,0:T(8,128)(2,1)} async-done(((bf16[64,4096]{1,0:T(8,128)(2,1)}), bf16[512,4096]{1,0:T(8,128)(2,1)}) %all-gather.5.cloned.1.call-update) | async-done | bytes 4194320 | tf_op jit(solution)/shard_map/all_gather | solution.py:25
  72.1 0.0 copy-start
  72.1 3.2 fusion
  75.3 0.0 copy-done.1
  75.3 0.2 copy-done
  75.5 3.6 %fusion.2 = bf16[512,4096]{1,0:T(8,128)(2,1)} fusion(bf16[512,4096]{1,0:T(8,128)(2,1)S(1)} %copy-done, f32[4096]{0:T(1024)S(1)} %copy-done.1, f32[512]{0:T(512)S(1)} %add_rsqrt_fusion), kind=kLoop, calls=%fused_computation.4 | loop fusion | flops 8388608 | bytes 8407040 | tf_op jit(solution)/shard_map/convert_element_type | solution.py:10
  79.1 80.9 %all-gather.9.cloned.1.call-done = bf16[128,32,512]{2,1,0:T(8,128)(2,1)} async-done(((bf16[2,32,512]{2,1,0:T(8,128)(2,1)}), bf16[128,32,512]{2,1,0:T(8,128)(2,1)}) %all-gather.9.cloned.1.call-update) | async-done | bytes 4194320 | tf_op jit(solution)/shard_map/all_gather | solution.py:38
  160.1 7.3 %fusion.5 = bf16[1,32,512]{2,0,1:T(2,128)(2,1)S(1)} fusion(bf16[128,32,512]{2,1,0:T(8,128)(2,1)} %all-gather.9.cloned.1.call-done, s32[]{:T(128)} %fusion.18), kind=kOutput, calls=%fused_computation.7 | convolution fusion | flops 4194432 | bytes 4227076 | tf_op jit(solution)/shard_map/qk,kcd->qcd/dot_general | solution.py:43
  167.4 1.3 convolution_bitcast_fusion
  168.6 24.1 %psum.7 = bf16[1,512,32]{1,2,0:T(8,128)(2,1)S(1)} all-reduce(f32[1,512,32]{1,2,0:T(8,128)S(1)} %convolution_bitcast_fusion), channel_id=1, replica_groups=mesh['req'=64,'tensor'=8] {'tensor'}, use_global_device_ids=true, to_apply=%region_2.3 | all-reduce | flops 16384 | bytes 98304 | tf_op jit(solution)/shard_map/psum | solution.py:54
  192.7 52.7 %all-gather.7.cloned.1.call-done = bf16[4096,512]{1,0:T(8,128)(2,1)} async-done(((bf16[64,512]{1,0:T(8,128)(2,1)}), bf16[4096,512]{1,0:T(8,128)(2,1)}) %all-gather.7.cloned.1.call-update) | async-done | bytes 4194320 | tf_op jit(solution)/shard_map/all_gather | solution.py:31
  245.4 5.8 %fusion.22 = f32[512,512]{1,0:T(8,128)S(1)} fusion(bf16[512,4096]{1,0:T(8,128)(2,1)} %fusion.2, bf16[4096,512]{1,0:T(8,128)(2,1)} %all-gather.7.cloned.1.call-done), kind=kOutput, calls=%fused_computation.31 | convolution fusion | flops 2147483648 | bytes 9437184 | tf_op jit(solution)/shard_map/dot_general | solution.py:29
  251.2 79.4 %all-gather.11.cloned.1.call-done = bf16[128,32,512]{2,1,0:T(8,128)(2,1)} async-done(((bf16[2,32,512]{2,1,0:T(8,128)(2,1)}), bf16[128,32,512]{2,1,0:T(8,128)(2,1)}) %all-gather.11.cloned.1.call-update) | async-done | bytes 4194320 | tf_op jit(solution)/shard_map/all_gather | solution.py:39
  330.6 7.3 %fusion.3 = bf16[1,32,512]{2,0,1:T(2,128)(2,1)S(1)} fusion(bf16[128,32,512]{2,1,0:T(8,128)(2,1)} %all-gather.11.cloned.1.call-done, s32[]{:T(128)} %fusion.18), kind=kOutput, calls=%fused_computation.5 | convolution fusion | flops 4194432 | bytes 4227076 | tf_op jit(solution)/shard_map/qk,kcd->qcd/dot_general | solution.py:44
  337.9 1.1 fusion.8
  (2 shorter events, 0.0 us)
Async XLA Ops:
  6.5 68.8 %copy-start.1 = (f32[4096]{0:T(1024)S(1)}, f32[4096]{0:T(1024)}, u32[]{:S(2)}) copy-start(f32[4096]{0:T(1024)} %param.9) | copy-start | bytes 49156
  6.5 65.6 %all-gather.5.cloned.1.call-start = ((), (), s32[]{:S(2)}) async-start(), calls=%async_computation | async-start | bytes 4718592 | tf_op jit(solution)/shard_map/all_gather | solution.py:25
  7.3 152.8 %all-gather.9.cloned.1.call-start = ((), (), s32[]{:S(2)}) async-start(), calls=%async_computation.2 | async-start | bytes 4259840 | tf_op jit(solution)/shard_map/all_gather | solution.py:38
  8.0 237.4 %all-gather.7.cloned.1.call-start = ((), (), s32[]{:S(2)}) async-start(), calls=%async_computation.1 | async-start | bytes 4259840 | tf_op jit(solution)/shard_map/all_gather | solution.py:31
  8.7 321.8 %all-gather.11.cloned.1.call-start = ((), (), s32[]{:S(2)}) async-start(), calls=%async_computation.3 | async-start | bytes 4259840 | tf_op jit(solution)/shard_map/all_gather | solution.py:39
  72.1 3.4 copy-start
Sparse Core Ops, SparseCore 0:
  9.4 62.6 all-gather.4
  75.4 84.5 all-gather.8
  163.4 81.9 all-gather.6
  248.6 81.9 all-gather.10
where the time goes:
time: 346 us
  waiting for transfers between devices  276 us (80%)
  blocking collectives  24.1 us (7%)
  matrix products  22.8 us (7%)
  between operations  14.4 us (4%)
  other arithmetic  8.11 us (2%)
    all_gather x1, waiting for transfers between devices, per_device(): lax.all_gather(adapter_down_weight, 'req', axis=0, tiled=True)  80.9 us
    all_gather x1, waiting for transfers between devices, per_device(): lax.all_gather(adapter_up_weight, 'req', axis=0, tiled=True)  79.4 us
    all_gather x1, waiting for transfers between devices, per_device(): whole = lax.all_gather(prompts, 'tensor', axis=0, tiled=True)  60.2 us
    all_gather x1, waiting for transfers between devices, per_device(): lax.all_gather(query_base_matrix, 'req', axis=0, tiled=True)  52.7 us
    psum x1, blocking collectives, per_device(): low = lax.psum(partial_value, 'tensor').astype(jnp.bfloat16)  24.1 us
    dot_general x1, matrix products, per_device(): jnp.einsum('qk,kcd->qcd', onehot, pieces[0], preferred_element_type=jnp.f...  7.31 us
    dot_general x1, matrix products, per_device(): jnp.einsum('qk,kcd->qcd', onehot, pieces[1], preferred_element_type=jnp.f...  7.31 us
  transfers between devices with their start and end apart: 4, of which 4 were waited for; matrix products, arithmetic and copies ran while one was open for 7% of the time, Pallas kernels for 0%

commit v1 on v0

v1 whole, which is shorter than its diff:
```python
import functools

import jax
import jax.numpy as jnp
from jax import lax
from jax.experimental import pallas as pl
from jax.experimental.pallas import tpu as pltpu
from jax.sharding import PartitionSpec as P

Z, X, C, Y = 8, 4, 2, 8
RING = (-3, 0, 3, -4, -1, 2, -2, 1)
QUAD = (0, -1, 1, 2)


def req_pairs(dz=0, dx=0, dc=0):
    return [
        ((z * X + x) * C + c, (((z + dz) % Z) * X + (x + dx) % X) * C + (c + dc) % C)
        for z in range(Z)
        for x in range(X)
        for c in range(C)
    ]


def shift(value, **by):
    return lax.ppermute(value, "req", req_pairs(**by))


def shift_y(value, by):
    return lax.ppermute(value, "tensor", [(y, (y + by) % Y) for y in range(Y)])


def ring_gather(value, move):
    trio = jnp.concatenate([move(value, 3), value, move(value, -3)], axis=0)
    n = value.shape[0]
    before = move(trio, 1)
    after = move(trio[: 2 * n], -1)
    return jnp.concatenate([trio, before, after], axis=0)


def normalize(rows, layer_norm_gain):
    values = rows.astype(jnp.float32)
    scale = lax.rsqrt(jnp.mean(values * values, axis=-1, keepdims=True) + 1e-06)
    return (values * scale * layer_norm_gain).astype(jnp.bfloat16)


def pick_kernel(place_ref, mine_ref, other_ref, minus_ref, plus_ref, own_ref, sems):
    outs = [(minus_ref, i) for i in range(3)] + [(plus_ref, i) for i in range(2)] + [(own_ref, i) for i in range(3)]
    for n, (ref, i) in enumerate(outs):
        side, at = place_ref[2 * n], place_ref[2 * n + 1]

        @pl.when(side == 0)
        def _(ref=ref, i=i, at=at, n=n):
            pltpu.make_async_copy(mine_ref.at[at], ref.at[i], sems.at[n]).start()

        @pl.when(side != 0)
        def _(ref=ref, i=i, at=at, n=n):
            pltpu.make_async_copy(other_ref.at[at], ref.at[i], sems.at[n]).start()

    for n, (ref, i) in enumerate(outs):
        pltpu.make_async_copy(mine_ref.at[0], ref.at[i], sems.at[n]).wait()


def project_kernel(at_ref, rows_ref, mine_ref, other_ref, down_ref, up_ref, out_ref, rows, weight, down, acc, row_sems, weight_sems, down_sems):
    z, x, c, y, length = (at_ref[i] for i in range(5))
    copies = []
    for j, dz in enumerate(RING):
        feature = lax.rem(z + dz + Z, Z)
        here = []
        for s, side in enumerate((mine_ref, other_ref)):
            for q, dx in enumerate(QUAD):
                to = lax.rem(x + dx + X, X) * C + lax.rem(c + s, C)
                here.append(
                    pltpu.make_async_copy(
                        side.at[pl.ds((q * Z + j) * 64, 64)],
                        weight.at[j, pl.ds(pl.multiple_of(to * 64, 64), 64)],
                        weight_sems.at[j * 8 + s * 4 + q],
                    )
                )
        here.append(
            pltpu.make_async_copy(
                rows_ref.at[:, pl.ds(pl.multiple_of(feature * 512, 512), 512)], rows.at[j], row_sems.at[j]
            )
        )
        for copy in here:
            copy.start()
        copies.append(here)
    down_copies = []
    for j, dy in enumerate(RING):
        to = lax.rem(y + dy + Y, Y)
        down_copies.append(pltpu.make_async_copy(down_ref.at[pl.ds(j * 32, 32)], down.at[to], down_sems.at[j]))
        down_copies[-1].start()
    for copy in down_copies:
        copy.wait()
    low = jnp.zeros((rows.shape[1], 32), jnp.float32)
    for j, dz in enumerate(RING):
        feature = lax.rem(z + dz + Z, Z)
        for copy in copies[j]:
            copy.wait()
        term = jnp.dot(rows[j], weight[j], preferred_element_type=jnp.float32)
        if j == 0:
            acc[...] = term
        else:
            acc[...] += term
        low += lax.dot_general(rows[j], down[feature], (((1,), (1,)), ((), ())), preferred_element_type=jnp.float32)
    total = acc[...] + jnp.dot(low.astype(jnp.bfloat16), up_ref[...], preferred_element_type=jnp.float32)
    valid = lax.broadcasted_iota(jnp.int32, total.shape, 0) < length
    out_ref[...] = jnp.where(valid, total, 0.0).astype(jnp.bfloat16)


def per_device(
    prompts,
    layer_norm_gain,
    query_base_matrix,
    adapter_down_weight,
    adapter_up_weight,
    request_prompt_length,
    request_adapter_ident,
    adapter_pool_row,
):
    req, y = lax.axis_index("req"), lax.axis_index("tensor")
    z, x, c = req // (X * C), (req // C) % X, req % C
    normed = lax.all_gather(normalize(prompts, layer_norm_gain), "tensor", axis=0, tiled=True)

    hits = request_adapter_ident[:, None] == jnp.arange(adapter_pool_row.shape[0], dtype=jnp.int32)[None, :]
    slot = jnp.sum(jnp.where(hits, adapter_pool_row[None, :], 0))

    noted = jnp.full((16, 512), slot, jnp.bfloat16)
    ring = ring_gather(jnp.concatenate([query_base_matrix, noted], axis=0), lambda v, k: shift(v, dz=k))
    ring = ring.reshape(Z, 80, 512)
    ring_slots = ring[:, 64, 0].astype(jnp.int32)
    wanted = {dz % Z: ring_slots[j] for j, dz in enumerate(RING)}
    weight = ring[:, :64].reshape(512, 512)
    from_left, from_right = shift(weight, dx=1), shift(weight, dx=-1)
    far_pairs = [p for p in req_pairs(dx=1) if p[0] % C == 0] + [p for p in req_pairs(dx=-1) if p[0] % C == 1]
    far = lax.ppermute(jnp.where(c == 0, from_left, from_right), "req", far_pairs)
    mine = jnp.concatenate([weight, from_left, from_right, far], axis=0)
    other = shift(mine, dc=1)

    own = jnp.concatenate([adapter_down_weight, adapter_up_weight], axis=1)
    plane = jnp.concatenate([own, shift(own, dx=1), shift(own, dx=-1), shift(own, dx=2)], axis=0)
    plane_other = shift(plane, dc=1)
    place = []
    for d in (-1, -4, 2, 1, -2, 0, 3, -3):
        s = wanted[d % Z]
        owner = (s // 2) % (X * C)
        dx = (owner // C - x) % X
        at = jnp.where(dx == 0, 0, jnp.where(dx == 3, 1, jnp.where(dx == 1, 2, 3))) * 2 + s % 2
        place += [(owner % C != c).astype(jnp.int32), at]
    slab = jax.ShapeDtypeStruct((3, 64, 512), jnp.bfloat16)
    minus, plus, kept = pl.pallas_call(
        pick_kernel,
        out_shape=(slab, jax.ShapeDtypeStruct((2, 64, 512), jnp.bfloat16), slab),
        in_specs=[pl.BlockSpec(memory_space=pltpu.SMEM)] + [pl.BlockSpec(memory_space=pl.ANY)] * 2,
        out_specs=[pl.BlockSpec(memory_space=pl.ANY)] * 3,
        scratch_shapes=[pltpu.SemaphoreType.DMA((8,))],
        name="pick_adapters",
    )(jnp.stack(place), plane, plane_other)
    above = shift(minus, dz=-1)
    below = shift(plus, dz=1)

    def nearest(d, own_part, below_part, above_part):
        rel = (wanted[d % Z] // (2 * X * C) - z) % Z
        return jnp.where(rel == 0, own_part, jnp.where(rel == 1, above_part, below_part))

    near = nearest(0, kept[0], below[0], above[0])
    to_plus = nearest(3, kept[1], above[2], above[2])
    to_minus = nearest(-3, kept[2], below[1], above[1])
    from_minus = shift(to_plus, dz=3)
    from_plus = shift(to_minus, dz=-3)
    gone = (z - wanted[0] // (2 * X * C)) % Z
    adapter = jnp.where((gone <= 1) | (gone == 7), near, jnp.where((gone == 2) | (gone == 3), from_minus, from_plus))
    down = ring_gather(adapter[:32], shift_y)

    at = jnp.stack([z, x, c, y, request_prompt_length[0]]).astype(jnp.int32)
    return pl.pallas_call(
        project_kernel,
        out_shape=jax.ShapeDtypeStruct((512, 512), jnp.bfloat16),
        in_specs=[pl.BlockSpec(memory_space=pltpu.SMEM)]
        + [pl.BlockSpec(memory_space=pl.ANY)] * 4
        + [pl.BlockSpec(memory_space=pltpu.VMEM)],
        out_specs=pl.BlockSpec(memory_space=pltpu.VMEM),
        scratch_shapes=[
            pltpu.VMEM((8, 512, 512), jnp.bfloat16),
            pltpu.VMEM((8, 512, 512), jnp.bfloat16),
            pltpu.VMEM((8, 32, 512), jnp.bfloat16),
            pltpu.VMEM((512, 512), jnp.float32),
            pltpu.SemaphoreType.DMA((8,)),
            pltpu.SemaphoreType.DMA((64,)),
            pltpu.SemaphoreType.DMA((8,)),
        ],
        compiler_params=pltpu.CompilerParams(vmem_limit_bytes=32 * 1024 * 1024),
        cost_estimate=pl.CostEstimate(flops=2 * 512 * 4096 * 544, bytes_accessed=9 << 20, transcendentals=0),
        name="project",
    )(at, normed, mine, other, down, adapter[32:])


def solution(mesh):
    in_specs = (
        P(("req", "tensor"), None),
        P(),
        P("req", "tensor"),
        P("req", None, "tensor"),
        P("req", None, "tensor"),
        P("req"),
        P("req"),
        P(),
    )
    out_specs = P("req", "tensor")
    return jax.shard_map(
        per_device, mesh=mesh, in_specs=in_specs, out_specs=out_specs, check_vma=False
    )
```

time: 346 us -> 204 us (0.59)
  the two profiles are of different devices: /device:TPU:1 before, /device:TPU:8 now
where the time goes in v1:
time: 204 us; the launch traced here: 202 us
  starting transfers between devices  73.5 us (36%)
  waiting for transfers between devices  46.5 us (23%)
  between operations  36.8 us (18%)
  Pallas kernels  29 us (14%)
  other arithmetic  10.4 us (5%)
  local copies, waits for them, and re-layouts  6.22 us (3%)
    ppermute x15, starting transfers between devices, shift(): return lax.ppermute(value, 'req', req_pairs(**by))  57.4 us
    ppermute x15, waiting for transfers between devices, shift(): return lax.ppermute(value, 'req', req_pairs(**by))  37.5 us
    pallas_call x1, Pallas kernels, per_device(): pl.pallas_call(pick_kernel, out_shape=(slab, jax.ShapeDtypeStruct((2, 64,...  17.7 us
    ppermute x4, starting transfers between devices, shift_y(): return lax.ppermute(value, 'tensor', [(y, (y + by) % Y) for y in range(Y)])  14.2 us
    pallas_call x1, Pallas kernels, per_device(): pl.pallas_call(project_kernel, out_shape=jax.ShapeDtypeStruct((512, 512),...  11.3 us
    ppermute x4, waiting for transfers between devices, shift_y(): return lax.ppermute(value, 'tensor', [(y, (y + by) % Y) for y in range(Y)])  8.96 us
  transfers between devices with their start and end apart: 21, of which 11 were waited for; matrix products, arithmetic and copies ran while one was open for 5% of the time, Pallas kernels for 9%

profile of v1, /device:TPU:8, one launch (start us, length us, event | category | flops | bytes accessed | tf_op | source)
XLA Modules:
  0.0 202.4 jit_solution(17784223950300106807)
XLA Ops:
  6.5 0.0 all-gather.2.cloned.1.call-start
  6.5 1.3 fusion
  7.8 2.0 %fusion.2 = bf16[64,4096]{1,0:T(8,128)(2,1)} fusion(bf16[64,4096]{1,0:T(8,128)(2,1)} %param.8, f32[4096]{0:T(1024)} %param.9, f32[64]{0:T(128)S(1)} %add_rsqrt_fusion), kind=kLoop, calls=%fused_computation.5 | loop fusion | flops 1048576 | bytes 1065216 | tf_op jit(solution)/shard_map/convert_element_type | solution.py:43
  9.9 0.0 all-gather.2.cloned.1.call-update
  10.5 1.4 fusion.9
  12.6 0.8 concatenate.33
  13.4 7.9 %collective-permute-start = (bf16[80,512]{1,0:T(8,128)(2,1)S(1)}, bf16[80,512]{1,0:T(8,128)(2,1)S(1)}, u32[]{:S(2)}, u32[]{:S(2)}) collective-permute-start(bf16[80,512]{1,0:T(8,128)(2,1)S(1)} %concatenate.33), channel_id=1, source_target_pairs={{0,192},{8,200},{16,208},{24,216},{32,224},{40,232},{48,240},{56,2... | collective-permute-start | bytes 245768 | tf_op jit(solution)/shard_map/ppermute | solution.py:25
  21.3 5.0 %collective-permute-start.1 = (bf16[80,512]{1,0:T(8,128)(2,1)S(1)}, bf16[80,512]{1,0:T(8,128)(2,1)S(1)}, u32[]{:S(2)}, u32[]{:S(2)}) collective-permute-start(bf16[80,512]{1,0:T(8,128)(2,1)S(1)} %concatenate.33), channel_id=1, source_target_pairs={{0,320},{8,328},{16,336},{24,344},{32,352},{40,360},{48,368},{56,3... | collective-permute-start | bytes 245768 | tf_op jit(solution)/shard_map/ppermute | solution.py:25
  26.3 0.7 collective-permute-done
  27.0 0.9 pad_maximum_fusion.3
  27.9 5.7 %collective-permute-start.3 = (bf16[160,512]{1,0:T(8,128)(2,1)S(1)}, bf16[160,512]{1,0:T(8,128)(2,1)S(1)}, u32[]{:S(2)}, u32[]{:S(2)}) collective-permute-start(bf16[160,512]{1,0:T(8,128)(2,1)S(1)} %pad_maximum_fusion.3), channel_id=1, source_target_pairs={{0,448},{8,456},{16,464},{24,472},{32,480},{40,488},{48,496},{56,5... | collective-permute-start | bytes 491528 | tf_op jit(solution)/shard_map/ppermute | solution.py:25
  33.6 0.0 collective-permute-done.1
  33.6 0.9 pad_maximum_fusion.2
  34.4 4.6 %collective-permute-start.2 = (bf16[240,512]{1,0:T(8,128)(2,1)S(1)}, bf16[240,512]{1,0:T(8,128)(2,1)S(1)}, u32[]{:S(2)}, u32[]{:S(2)}) collective-permute-start(bf16[240,512]{1,0:T(8,128)(2,1)S(1)} %pad_maximum_fusion.2), channel_id=1, source_target_pairs={{0,64},{8,72},{16,80},{24,88},{32,96},{40,104},{48,112},{56,120},{... | collective-permute-start | bytes 737288 | tf_op jit(solution)/shard_map/ppermute | solution.py:25
  39.1 0.8 constant_dynamic-update-slice_fusion.4
  40.0 7.0 %collective-permute-done.2 = bf16[240,512]{1,0:T(8,128)(2,1)S(1)} collective-permute-done((bf16[240,512]{1,0:T(8,128)(2,1)S(1)}, bf16[240,512]{1,0:T(8,128)(2,1)S(1)}, u32[]{:S(2)}, u32[]{:S(2)}) %collective-permute-start.2) | collective-permute-done | bytes 245792 | tf_op jit(solution)/shard_map/ppermute | solution.py:25
  47.0 0.0 collective-permute-done.3
  47.1 0.0 copy-start.4
  47.1 0.8 copy-done.4
  47.9 4.7 %collective-permute-start.5 = (bf16[512,512]{1,0:T(8,128)(2,1)S(1)}, bf16[512,512]{1,0:T(8,128)(2,1)S(1)}, u32[]{:S(2)}, u32[]{:S(2)}) collective-permute-start(bf16[512,512]{1,0:T(8,128)(2,1)S(1)} %bitcast.40), channel_id=1, source_target_pairs={{0,48},{8,56},{16,0},{24,8},{32,16},{40,24},{48,32},{56,40},{64,11... | collective-permute-start | bytes 1572872 | tf_op jit(solution)/shard_map/ppermute | solution.py:25
  52.6 1.9 collective-permute-start.4
  54.5 8.5 %collective-permute-done.5 = bf16[512,512]{1,0:T(8,128)(2,1)S(1)} collective-permute-done((bf16[512,512]{1,0:T(8,128)(2,1)S(1)}, bf16[512,512]{1,0:T(8,128)(2,1)S(1)}, u32[]{:S(2)}, u32[]{:S(2)}) %collective-permute-start.5) | collective-permute-done | bytes 524320 | tf_op jit(solution)/shard_map/ppermute | solution.py:25
  63.1 5.3 %collective-permute-done.4 = bf16[512,512]{1,0:T(8,128)(2,1)S(1)} collective-permute-done((bf16[512,512]{1,0:T(8,128)(2,1)S(1)}, bf16[512,512]{1,0:T(8,128)(2,1)S(1)}, u32[]{:S(2)}, u32[]{:S(2)}) %collective-permute-start.4) | collective-permute-done | bytes 524320 | tf_op jit(solution)/shard_map/ppermute | solution.py:25
  68.4 0.1 broadcast_select_fusion
  68.5 1.9 collective-permute-start.6
  70.4 3.0 %collective-permute-start.10 = (bf16[2,64,512]{2,1,0:T(8,128)(2,1)S(1)}, bf16[2,64,512]{2,1,0:T(8,128)(2,1)S(1)}, u32[]{:S(2)}, u32[]{:S(2)}) collective-permute-start(bf16[2,64,512]{2,1,0:T(8,128)(2,1)S(1)} %constant_dynamic-update-slice_fusion.6), channel_id=1, source_target_pairs={{0,32},{8,40},{16,48},{24,56},{32,0},{40,8},{48,16},{56,24},{64,96... | collective-permute-start | bytes 393224 | tf_op jit(solution)/shard_map/ppermute | solution.py:25
  73.4 4.1 %collective-permute-start.9 = (bf16[2,64,512]{2,1,0:T(8,128)(2,1)S(1)}, bf16[2,64,512]{2,1,0:T(8,128)(2,1)S(1)}, u32[]{:S(2)}, u32[]{:S(2)}) collective-permute-start(bf16[2,64,512]{2,1,0:T(8,128)(2,1)S(1)} %constant_dynamic-update-slice_fusion.6), channel_id=1, source_target_pairs={{0,48},{8,56},{16,0},{24,8},{32,16},{40,24},{48,32},{56,40},{64,11... | collective-permute-start | bytes 393224 | tf_op jit(solution)/shard_map/ppermute | solution.py:25
  77.5 2.8 %collective-permute-start.8 = (bf16[2,64,512]{2,1,0:T(8,128)(2,1)S(1)}, bf16[2,64,512]{2,1,0:T(8,128)(2,1)S(1)}, u32[]{:S(2)}, u32[]{:S(2)}) collective-permute-start(bf16[2,64,512]{2,1,0:T(8,128)(2,1)S(1)} %constant_dynamic-update-slice_fusion.6), channel_id=1, source_target_pairs={{0,16},{8,24},{16,32},{24,40},{32,48},{40,56},{48,0},{56,8},{64,80... | collective-permute-start | bytes 393224 | tf_op jit(solution)/shard_map/ppermute | solution.py:25
  80.3 2.2 %collective-permute-done.10 = bf16[2,64,512]{2,1,0:T(8,128)(2,1)S(1)} collective-permute-done((bf16[2,64,512]{2,1,0:T(8,128)(2,1)S(1)}, bf16[2,64,512]{2,1,0:T(8,128)(2,1)S(1)}, u32[]{:S(2)}, u32[]{:S(2)}) %collective-permute-start.10) | collective-permute-done | bytes 131104 | tf_op jit(solution)/shard_map/ppermute | solution.py:25
  82.4 0.0 collective-permute-done.9
  82.5 3.6 %collective-permute-done.8 = bf16[2,64,512]{2,1,0:T(8,128)(2,1)S(1)} collective-permute-done((bf16[2,64,512]{2,1,0:T(8,128)(2,1)S(1)}, bf16[2,64,512]{2,1,0:T(8,128)(2,1)S(1)}, u32[]{:S(2)}, u32[]{:S(2)}) %collective-permute-start.8) | collective-permute-done | bytes 131104 | tf_op jit(solution)/shard_map/ppermute | solution.py:25
  86.0 0.1 pad_maximum_fusion.1.mine_ref
  86.1 1.9 collective-permute-start.11
  88.1 0.0 collective-permute-done.6
  88.1 1.3 pad_maximum_fusion.mine_ref
  89.4 2.4 %collective-permute-start.7 = (bf16[2048,512]{1,0:T(8,128)(2,1)S(1)}, bf16[2048,512]{1,0:T(8,128)(2,1)}, u32[]{:S(2)}, u32[]{:S(2)}) collective-permute-start(bf16[2048,512]{1,0:T(8,128)(2,1)S(1)} %pad_maximum_fusion.mine_ref), channel_id=1, source_target_pairs={{0,8},{8,0},{16,24},{24,16},{32,40},{40,32},{48,56},{56,48},{64,72... | collective-permute-start | bytes 6291464 | tf_op jit(solution)/shard_map/ppermute | solution.py:25
  91.9 0.7 slice_convert_fusion
  92.6 0.6 fusion.11
  113.9 0.7 stack.119.place_ref
  114.6 0.0 collective-permute-done.11.other_ref
  114.6 17.7 %pick_adapters.1 = (bf16[3,64,512]{2,1,0:T(8,128)(2,1)}, bf16[2,64,512]{2,1,0:T(8,128)(2,1)}, bf16[3,64,512]{2,1,0:T(8,128)(2,1)}) custom-call(s32[16]{0:T(128)} %stack.119.place_ref, bf16[8,64,512]{2,1,0:T(8,128)(2,1)} %copy-done.1, bf16[8,64,512]{2,1,0:T(8,128)(2,1)} %collective-permute-done.11.other_ref), custom_call_target="tpu_custom_call" | custom-call | tf_op jit(solution)/shard_map/pick_adapters/pallas_call | solution.py:150
  132.4 3.3 %collective-permute-start.12 = (bf16[3,64,512]{2,1,0:T(8,128)(2,1)}, bf16[3,64,512]{2,1,0:T(8,128)(2,1)S(1)}, u32[]{:S(2)}, u32[]{:S(2)}) collective-permute-start(bf16[3,64,512]{2,1,0:T(8,128)(2,1)} %get-tuple-element.9), channel_id=1, source_target_pairs={{0,448},{8,456},{16,464},{24,472},{32,480},{40,488},{48,496},{56,5... | collective-permute-start | bytes 589832 | tf_op jit(solution)/shard_map/ppermute | solution.py:25
  135.7 2.5 %collective-permute-start.13 = (bf16[2,64,512]{2,1,0:T(8,128)(2,1)}, bf16[2,64,512]{2,1,0:T(8,128)(2,1)S(1)}, u32[]{:S(2)}, u32[]{:S(2)}) collective-permute-start(bf16[2,64,512]{2,1,0:T(8,128)(2,1)} %get-tuple-element.10), channel_id=1, source_target_pairs={{0,64},{8,72},{16,80},{24,88},{32,96},{40,104},{48,112},{56,120},{... | collective-permute-start | bytes 393224 | tf_op jit(solution)/shard_map/ppermute | solution.py:25
  138.3 5.8 %collective-permute-done.13 = bf16[2,64,512]{2,1,0:T(8,128)(2,1)S(1)} collective-permute-done((bf16[2,64,512]{2,1,0:T(8,128)(2,1)}, bf16[2,64,512]{2,1,0:T(8,128)(2,1)S(1)}, u32[]{:S(2)}, u32[]{:S(2)}) %collective-permute-start.13) | collective-permute-done | bytes 131104 | tf_op jit(solution)/shard_map/ppermute | solution.py:25
  144.1 0.0 collective-permute-done.12
  144.1 0.9 fusion.4
  145.0 2.2 %collective-permute-start.15 = (bf16[64,512]{1,0:T(8,128)(2,1)S(1)}, bf16[64,512]{1,0:T(8,128)(2,1)S(1)}, u32[]{:S(2)}, u32[]{:S(2)}) collective-permute-start(bf16[64,512]{1,0:T(8,128)(2,1)S(1)} %get-tuple-element.11), channel_id=1, source_target_pairs={{0,320},{8,328},{16,336},{24,344},{32,352},{40,360},{48,368},{56,3... | collective-permute-start | bytes 196616 | tf_op jit(solution)/shard_map/ppermute | solution.py:25
  147.2 5.4 %collective-permute-start.14 = (bf16[64,512]{1,0:T(8,128)(2,1)S(1)}, bf16[64,512]{1,0:T(8,128)(2,1)S(1)}, u32[]{:S(2)}, u32[]{:S(2)}) collective-permute-start(bf16[64,512]{1,0:T(8,128)(2,1)S(1)} %get-tuple-element.12), channel_id=1, source_target_pairs={{0,192},{8,200},{16,208},{24,216},{32,224},{40,232},{48,240},{56,2... | collective-permute-start | bytes 196616 | tf_op jit(solution)/shard_map/ppermute | solution.py:25
  152.8 1.6 collective-permute-done.15
  154.4 2.7 %collective-permute-done.14 = bf16[64,512]{1,0:T(8,128)(2,1)S(1)} collective-permute-done((bf16[64,512]{1,0:T(8,128)(2,1)S(1)}, bf16[64,512]{1,0:T(8,128)(2,1)S(1)}, u32[]{:S(2)}, u32[]{:S(2)}) %collective-permute-start.14) | collective-permute-done | bytes 65568 | tf_op jit(solution)/shard_map/ppermute | solution.py:25
  157.1 0.9 fusion.8
  158.0 7.5 %collective-permute-start.16 = (bf16[32,512]{1,0:T(8,128)(2,1)S(1)}, bf16[32,512]{1,0:T(8,128)(2,1)S(1)}, u32[]{:S(2)}, u32[]{:S(2)}) collective-permute-start(bf16[32,512]{1,0:T(8,128)(2,1)S(1)} %slice.108), channel_id=1, source_target_pairs={{0,3},{1,4},{2,5},{3,6},{4,7},{5,0},{6,1},{7,2},{8,11},{9,12},{10,... | collective-permute-start | bytes 98312 | tf_op jit(solution)/shard_map/ppermute | solution.py:29
  166.1 0.1 stack.94.at_ref
  166.2 1.9 collective-permute-start.17
  168.1 0.0 collective-permute-done.16
  168.2 2.6 %collective-permute-start.19 = (bf16[64,512]{1,0:T(8,128)(2,1)S(1)}, bf16[64,512]{1,0:T(8,128)(2,1)S(1)}, u32[]{:S(2)}, u32[]{:S(2)}) collective-permute-start(bf16[64,512]{1,0:T(8,128)(2,1)S(1)} %pad_maximum_fusion.5), channel_id=1, source_target_pairs={{0,7},{1,0},{2,1},{3,2},{4,3},{5,4},{6,5},{7,6},{8,15},{9,8},{10,9... | collective-permute-start | bytes 196616 | tf_op jit(solution)/shard_map/ppermute | solution.py:29
  170.8 4.7 %collective-permute-done.17 = bf16[32,512]{1,0:T(8,128)(2,1)S(1)} collective-permute-done((bf16[32,512]{1,0:T(8,128)(2,1)S(1)}, bf16[32,512]{1,0:T(8,128)(2,1)S(1)}, u32[]{:S(2)}, u32[]{:S(2)}) %collective-permute-start.17) | collective-permute-done | bytes 32800 | tf_op jit(solution)/shard_map/ppermute | solution.py:29
  175.4 2.2 %collective-permute-start.18 = (bf16[96,512]{1,0:T(8,128)(2,1)S(1)}, bf16[96,512]{1,0:T(8,128)(2,1)S(1)}, u32[]{:S(2)}, u32[]{:S(2)}) collective-permute-start(bf16[96,512]{1,0:T(8,128)(2,1)S(1)} %pad_maximum_fusion.4), channel_id=1, source_target_pairs={{0,1},{1,2},{2,3},{3,4},{4,5},{5,6},{6,7},{7,0},{8,9},{9,10},{10,1... | collective-permute-start | bytes 294920 | tf_op jit(solution)/shard_map/ppermute | solution.py:29
  177.7 4.3 %collective-permute-done.18 = bf16[96,512]{1,0:T(8,128)(2,1)S(1)} collective-permute-done((bf16[96,512]{1,0:T(8,128)(2,1)S(1)}, bf16[96,512]{1,0:T(8,128)(2,1)S(1)}, u32[]{:S(2)}, u32[]{:S(2)}) %collective-permute-start.18) | collective-permute-done | bytes 98336 | tf_op jit(solution)/shard_map/ppermute | solution.py:29
  182.0 0.0 collective-permute-done.19
  182.0 0.0 collective-permute-done.7.other_ref
  182.0 0.0 all-gather.2.cloned.1.call-done.rows_ref
  182.0 2.2 %copy-done = bf16[512,4096]{1,0:T(8,128)(2,1)S(1)} copy-done((bf16[512,4096]{1,0:T(8,128)(2,1)S(1)}, bf16[512,4096]{1,0:T(8,128)(2,1)}, u32[]{:S(2)}) %copy-start) | copy-done | bytes 4194328
  184.2 11.3 %project.1 = bf16[512,512]{1,0:T(8,128)(2,1)} custom-call(s32[5]{0:T(128)S(1)} %stack.94.at_ref, bf16[512,4096]{1,0:T(8,128)(2,1)S(1)} %copy-done, bf16[2048,512]{1,0:T(8,128)(2,1)S(1)} %pad_maximum_fusion.mine_ref, bf16[2048,512]{1,0:T(8,128)(2,1)} %collective-permute-done.7.other_ref, bf16[256,512]{1,0:T(8,128)(2,1)S(1)} %constant_dynamic-update-slice_fusion.8.down_ref, ...), custom_call_target="tpu_custom_call" | custom-call | flops 2281701376 | bytes 9437184 | tf_op jit(solution)/shard_map/project/pallas_call | solution.py:175
  (29 shorter events, 0.2 us)
Async XLA Ops:
  6.5 63.9 %copy-start.5 = (bf16[2,32,512]{2,1,0:T(8,128)(2,1)S(1)}, bf16[2,32,512]{2,1,0:T(8,128)(2,1)}, u32[]{:S(2)}) copy-start(bf16[2,32,512]{2,1,0:T(8,128)(2,1)} %param.11) | copy-start | bytes 196612
  6.5 63.9 %copy-start.6 = (bf16[2,32,512]{2,1,0:T(8,128)(2,1)S(1)}, bf16[2,32,512]{2,1,0:T(8,128)(2,1)}, u32[]{:S(2)}) copy-start(bf16[2,32,512]{2,1,0:T(8,128)(2,1)} %param.12) | copy-start | bytes 196612
  6.5 175.5 %all-gather.2.cloned.1.call-start = ((), (), s32[]{:S(2)}) async-start(), calls=%async_computation | async-start | bytes 4718592 | tf_op jit(solution)/shard_map/all_gather | solution.py:122
  13.4 13.5 %collective-permute-start = (bf16[80,512]{1,0:T(8,128)(2,1)S(1)}, bf16[80,512]{1,0:T(8,128)(2,1)S(1)}, u32[]{:S(2)}, u32[]{:S(2)}) collective-permute-start(bf16[80,512]{1,0:T(8,128)(2,1)S(1)} %concatenate.33), channel_id=1, source_target_pairs={{0,192},{8,200},{16,208},{24,216},{32,224},{40,232},{48,240},{56,2... | collective-permute-start | bytes 245768 | tf_op jit(solution)/shard_map/ppermute | solution.py:25
  21.3 12.2 %collective-permute-start.1 = (bf16[80,512]{1,0:T(8,128)(2,1)S(1)}, bf16[80,512]{1,0:T(8,128)(2,1)S(1)}, u32[]{:S(2)}, u32[]{:S(2)}) collective-permute-start(bf16[80,512]{1,0:T(8,128)(2,1)S(1)} %concatenate.33), channel_id=1, source_target_pairs={{0,320},{8,328},{16,336},{24,344},{32,352},{40,360},{48,368},{56,3... | collective-permute-start | bytes 245768 | tf_op jit(solution)/shard_map/ppermute | solution.py:25
  27.9 19.2 %collective-permute-start.3 = (bf16[160,512]{1,0:T(8,128)(2,1)S(1)}, bf16[160,512]{1,0:T(8,128)(2,1)S(1)}, u32[]{:S(2)}, u32[]{:S(2)}) collective-permute-start(bf16[160,512]{1,0:T(8,128)(2,1)S(1)} %pad_maximum_fusion.3), channel_id=1, source_target_pairs={{0,448},{8,456},{16,464},{24,472},{32,480},{40,488},{48,496},{56,5... | collective-permute-start | bytes 491528 | tf_op jit(solution)/shard_map/ppermute | solution.py:25
  34.4 12.6 %collective-permute-start.2 = (bf16[240,512]{1,0:T(8,128)(2,1)S(1)}, bf16[240,512]{1,0:T(8,128)(2,1)S(1)}, u32[]{:S(2)}, u32[]{:S(2)}) collective-permute-start(bf16[240,512]{1,0:T(8,128)(2,1)S(1)} %pad_maximum_fusion.2), channel_id=1, source_target_pairs={{0,64},{8,72},{16,80},{24,88},{32,96},{40,104},{48,112},{56,120},{... | collective-permute-start | bytes 737288 | tf_op jit(solution)/shard_map/ppermute | solution.py:25
  47.1 0.9 copy-start.4
  47.9 15.2 %collective-permute-start.5 = (bf16[512,512]{1,0:T(8,128)(2,1)S(1)}, bf16[512,512]{1,0:T(8,128)(2,1)S(1)}, u32[]{:S(2)}, u32[]{:S(2)}) collective-permute-start(bf16[512,512]{1,0:T(8,128)(2,1)S(1)} %bitcast.40), channel_id=1, source_target_pairs={{0,48},{8,56},{16,0},{24,8},{32,16},{40,24},{48,32},{56,40},{64,11... | collective-permute-start | bytes 1572872 | tf_op jit(solution)/shard_map/ppermute | solution.py:25
  52.6 15.8 %collective-permute-start.4 = (bf16[512,512]{1,0:T(8,128)(2,1)S(1)}, bf16[512,512]{1,0:T(8,128)(2,1)S(1)}, u32[]{:S(2)}, u32[]{:S(2)}) collective-permute-start(bf16[512,512]{1,0:T(8,128)(2,1)S(1)} %bitcast.41), channel_id=1, source_target_pairs={{0,16},{8,24},{16,32},{24,40},{32,48},{40,56},{48,0},{56,8},{64,80... | collective-permute-start | bytes 1572872 | tf_op jit(solution)/shard_map/ppermute | solution.py:25
  63.1 25.0 %copy-start.2 = (bf16[512,512]{1,0:T(8,128)(2,1)}, bf16[512,512]{1,0:T(8,128)(2,1)S(1)}, u32[]{:S(2)}) copy-start(bf16[512,512]{1,0:T(8,128)(2,1)S(1)} %collective-permute-done.5) | copy-start | bytes 1572868
  68.4 19.6 %copy-start.3 = (bf16[512,512]{1,0:T(8,128)(2,1)}, bf16[512,512]{1,0:T(8,128)(2,1)S(1)}, u32[]{:S(2)}) copy-start(bf16[512,512]{1,0:T(8,128)(2,1)S(1)} %collective-permute-done.4) | copy-start | bytes 1572868
  68.5 19.6 %collective-permute-start.6 = (bf16[512,512]{1,0:T(8,128)(2,1)S(1)}, bf16[512,512]{1,0:T(8,128)(2,1)S(1)}, u32[]{:S(2)}, u32[]{:S(2)}) collective-permute-start(bf16[512,512]{1,0:T(8,128)(2,1)S(1)} %broadcast_select_fusion), channel_id=1, source_target_pairs={{0,16},{16,32},{32,48},{48,0},{64,80},{80,96},{96,112},{112,64},{1... | collective-permute-start | bytes 1572872 | tf_op jit(solution)/shard_map/ppermute | solution.py:135
  70.4 12.0 %collective-permute-start.10 = (bf16[2,64,512]{2,1,0:T(8,128)(2,1)S(1)}, bf16[2,64,512]{2,1,0:T(8,128)(2,1)S(1)}, u32[]{:S(2)}, u32[]{:S(2)}) collective-permute-start(bf16[2,64,512]{2,1,0:T(8,128)(2,1)S(1)} %constant_dynamic-update-slice_fusion.6), channel_id=1, source_target_pairs={{0,32},{8,40},{16,48},{24,56},{32,0},{40,8},{48,16},{56,24},{64,96... | collective-permute-start | bytes 393224 | tf_op jit(solution)/shard_map/ppermute | solution.py:25
  73.4 9.0 %collective-permute-start.9 = (bf16[2,64,512]{2,1,0:T(8,128)(2,1)S(1)}, bf16[2,64,512]{2,1,0:T(8,128)(2,1)S(1)}, u32[]{:S(2)}, u32[]{:S(2)}) collective-permute-start(bf16[2,64,512]{2,1,0:T(8,128)(2,1)S(1)} %constant_dynamic-update-slice_fusion.6), channel_id=1, source_target_pairs={{0,48},{8,56},{16,0},{24,8},{32,16},{40,24},{48,32},{56,40},{64,11... | collective-permute-start | bytes 393224 | tf_op jit(solution)/shard_map/ppermute | solution.py:25
  77.5 8.5 %collective-permute-start.8 = (bf16[2,64,512]{2,1,0:T(8,128)(2,1)S(1)}, bf16[2,64,512]{2,1,0:T(8,128)(2,1)S(1)}, u32[]{:S(2)}, u32[]{:S(2)}) collective-permute-start(bf16[2,64,512]{2,1,0:T(8,128)(2,1)S(1)} %constant_dynamic-update-slice_fusion.6), channel_id=1, source_target_pairs={{0,16},{8,24},{16,32},{24,40},{32,48},{40,56},{48,0},{56,8},{64,80... | collective-permute-start | bytes 393224 | tf_op jit(solution)/shard_map/ppermute | solution.py:25
  86.1 28.5 %copy-start.1 = (bf16[8,64,512]{2,1,0:T(8,128)(2,1)}, bf16[8,64,512]{2,1,0:T(8,128)(2,1)S(1)}, u32[]{:S(2)}) copy-start(bf16[8,64,512]{2,1,0:T(8,128)(2,1)S(1)} %pad_maximum_fusion.1.mine_ref) | copy-start | bytes 1572868
  86.1 28.5 %collective-permute-start.11 = (bf16[8,64,512]{2,1,0:T(8,128)(2,1)S(1)}, bf16[8,64,512]{2,1,0:T(8,128)(2,1)}, u32[]{:S(2)}, u32[]{:S(2)}) collective-permute-start(bf16[8,64,512]{2,1,0:T(8,128)(2,1)S(1)} %pad_maximum_fusion.1.mine_ref), channel_id=1, source_target_pairs={{0,8},{8,0},{16,24},{24,16},{32,40},{40,32},{48,56},{56,48},{64,72... | collective-permute-start | bytes 1572872 | tf_op jit(solution)/shard_map/ppermute | solution.py:25
  89.4 92.6 %collective-permute-start.7 = (bf16[2048,512]{1,0:T(8,128)(2,1)S(1)}, bf16[2048,512]{1,0:T(8,128)(2,1)}, u32[]{:S(2)}, u32[]{:S(2)}) collective-permute-start(bf16[2048,512]{1,0:T(8,128)(2,1)S(1)} %pad_maximum_fusion.mine_ref), channel_id=1, source_target_pairs={{0,8},{8,0},{16,24},{24,16},{32,40},{40,32},{48,56},{56,48},{64,72... | collective-permute-start | bytes 6291464 | tf_op jit(solution)/shard_map/ppermute | solution.py:25
  132.4 11.8 %collective-permute-start.12 = (bf16[3,64,512]{2,1,0:T(8,128)(2,1)}, bf16[3,64,512]{2,1,0:T(8,128)(2,1)S(1)}, u32[]{:S(2)}, u32[]{:S(2)}) collective-permute-start(bf16[3,64,512]{2,1,0:T(8,128)(2,1)} %get-tuple-element.9), channel_id=1, source_target_pairs={{0,448},{8,456},{16,464},{24,472},{32,480},{40,488},{48,496},{56,5... | collective-permute-start | bytes 589832 | tf_op jit(solution)/shard_map/ppermute | solution.py:25
  135.7 8.4 %collective-permute-start.13 = (bf16[2,64,512]{2,1,0:T(8,128)(2,1)}, bf16[2,64,512]{2,1,0:T(8,128)(2,1)S(1)}, u32[]{:S(2)}, u32[]{:S(2)}) collective-permute-start(bf16[2,64,512]{2,1,0:T(8,128)(2,1)} %get-tuple-element.10), channel_id=1, source_target_pairs={{0,64},{8,72},{16,80},{24,88},{32,96},{40,104},{48,112},{56,120},{... | collective-permute-start | bytes 393224 | tf_op jit(solution)/shard_map/ppermute | solution.py:25
  145.0 9.3 %collective-permute-start.15 = (bf16[64,512]{1,0:T(8,128)(2,1)S(1)}, bf16[64,512]{1,0:T(8,128)(2,1)S(1)}, u32[]{:S(2)}, u32[]{:S(2)}) collective-permute-start(bf16[64,512]{1,0:T(8,128)(2,1)S(1)} %get-tuple-element.11), channel_id=1, source_target_pairs={{0,320},{8,328},{16,336},{24,344},{32,352},{40,360},{48,368},{56,3... | collective-permute-start | bytes 196616 | tf_op jit(solution)/shard_map/ppermute | solution.py:25
  147.2 9.8 %collective-permute-start.14 = (bf16[64,512]{1,0:T(8,128)(2,1)S(1)}, bf16[64,512]{1,0:T(8,128)(2,1)S(1)}, u32[]{:S(2)}, u32[]{:S(2)}) collective-permute-start(bf16[64,512]{1,0:T(8,128)(2,1)S(1)} %get-tuple-element.12), channel_id=1, source_target_pairs={{0,192},{8,200},{16,208},{24,216},{32,224},{40,232},{48,240},{56,2... | collective-permute-start | bytes 196616 | tf_op jit(solution)/shard_map/ppermute | solution.py:25
  158.0 10.2 %collective-permute-start.16 = (bf16[32,512]{1,0:T(8,128)(2,1)S(1)}, bf16[32,512]{1,0:T(8,128)(2,1)S(1)}, u32[]{:S(2)}, u32[]{:S(2)}) collective-permute-start(bf16[32,512]{1,0:T(8,128)(2,1)S(1)} %slice.108), channel_id=1, source_target_pairs={{0,3},{1,4},{2,5},{3,6},{4,7},{5,0},{6,1},{7,2},{8,11},{9,12},{10,... | collective-permute-start | bytes 98312 | tf_op jit(solution)/shard_map/ppermute | solution.py:29
  166.2 9.2 %collective-permute-start.17 = (bf16[32,512]{1,0:T(8,128)(2,1)S(1)}, bf16[32,512]{1,0:T(8,128)(2,1)S(1)}, u32[]{:S(2)}, u32[]{:S(2)}) collective-permute-start(bf16[32,512]{1,0:T(8,128)(2,1)S(1)} %slice.108), channel_id=1, source_target_pairs={{0,5},{1,6},{2,7},{3,0},{4,1},{5,2},{6,3},{7,4},{8,13},{9,14},{10,... | collective-permute-start | bytes 98312 | tf_op jit(solution)/shard_map/ppermute | solution.py:29
  168.2 13.8 %collective-permute-start.19 = (bf16[64,512]{1,0:T(8,128)(2,1)S(1)}, bf16[64,512]{1,0:T(8,128)(2,1)S(1)}, u32[]{:S(2)}, u32[]{:S(2)}) collective-permute-start(bf16[64,512]{1,0:T(8,128)(2,1)S(1)} %pad_maximum_fusion.5), channel_id=1, source_target_pairs={{0,7},{1,0},{2,1},{3,2},{4,3},{5,4},{6,5},{7,6},{8,15},{9,8},{10,9... | collective-permute-start | bytes 196616 | tf_op jit(solution)/shard_map/ppermute | solution.py:29
  175.4 6.5 %collective-permute-start.18 = (bf16[96,512]{1,0:T(8,128)(2,1)S(1)}, bf16[96,512]{1,0:T(8,128)(2,1)S(1)}, u32[]{:S(2)}, u32[]{:S(2)}) collective-permute-start(bf16[96,512]{1,0:T(8,128)(2,1)S(1)} %pad_maximum_fusion.4), channel_id=1, source_target_pairs={{0,1},{1,2},{2,3},{3,4},{4,5},{5,6},{6,7},{7,0},{8,9},{9,10},{10,1... | collective-permute-start | bytes 294920 | tf_op jit(solution)/shard_map/ppermute | solution.py:29
  182.0 2.2 %copy-start = (bf16[512,4096]{1,0:T(8,128)(2,1)S(1)}, bf16[512,4096]{1,0:T(8,128)(2,1)}, u32[]{:S(2)}) copy-start(bf16[512,4096]{1,0:T(8,128)(2,1)} %all-gather.2.cloned.1.call-done.rows_ref) | copy-start | bytes 12582916
Sparse Core Ops, SparseCore 0:
  10.0 60.3 all-gather.1

commit v2 on v0

v2 whole, which is shorter than its diff:
```python
import jax
import jax.numpy as jnp
from jax import lax
from jax.experimental import pallas as pl
from jax.experimental.pallas import tpu as pltpu
from jax.sharding import PartitionSpec as P

RING = (-3, 0, 3, -4, -1, 2, -2, 1)
QUAD = (0, -1, 1, 2)
Z, X, C, Y = 8, 4, 2, 8
REQ = ("z", "x", "c")


def after(value, *others):
    return lax.optimization_barrier((value, *others))[0]


def to_all(value, axis, size):
    return lax.all_to_all(jnp.broadcast_to(value, (size, *value.shape)), axis, 0, 0)


def req_pairs(dz=0, dx=0):
    return [
        ((z * X + x) * C + c, (((z + dz) % Z) * X + (x + dx) % X) * C + c)
        for z in range(Z)
        for x in range(X)
        for c in range(C)
    ]


def shift(value, **by):
    return lax.ppermute(value, REQ, req_pairs(**by))


def shift_y(value, by):
    return lax.ppermute(value, "y", [(y, (y + by) % Y) for y in range(Y)])


def swap(value):
    return lax.ppermute(value, "c", [(0, 1), (1, 0)])


def prepare_kernel(ident_ref, pool_ref, rows_ref, gain_ref, base_ref, down_ref, up_ref, rows_out, base_out, pair_out):
    base_out[:64] = base_ref[...]
    base_out[64:] = jnp.full((16, 512), pool_ref[ident_ref[0]].astype(jnp.float32)).astype(jnp.bfloat16)
    values = rows_ref[...].astype(jnp.float32)
    scale = lax.rsqrt(jnp.mean(values * values, axis=-1, keepdims=True) + 1e-06)
    rows_out[...] = (values * scale * gain_ref[...]).astype(jnp.bfloat16)
    pair_out[:, :32] = down_ref[...]
    pair_out[:, 32:] = up_ref[...]


def pick_kernel(slots_ref, mine_ref, other_ref, out_ref):
    z, c = lax.axis_index("z"), lax.axis_index("c")
    for j, dz in enumerate(RING):
        slot = slots_ref[j]
        owner = lax.rem(lax.div(slot, 2), X * C)
        at = lax.div(owner, C) * 2 + lax.rem(slot, 2)
        to = lax.rem(z + dz + Z, Z)

        @pl.when(lax.rem(owner, C) == c)
        def _(to=to, at=at):
            out_ref[to] = mine_ref[at]

        @pl.when(lax.rem(owner, C) != c)
        def _(to=to, at=at):
            out_ref[to] = other_ref[at]


def bf16(*shape):
    return jax.ShapeDtypeStruct(shape, jnp.bfloat16)


def small(kernel, name, out_shape, scalars, *arrays):
    smem, vmem = pl.BlockSpec(memory_space=pltpu.SMEM), pl.BlockSpec(memory_space=pltpu.VMEM)
    return pl.pallas_call(
        kernel,
        out_shape=out_shape,
        in_specs=[smem] * len(scalars) + [vmem] * len(arrays),
        out_specs=[vmem] * len(out_shape),
        cost_estimate=pl.CostEstimate(flops=0, bytes_accessed=2 << 20, transcendentals=0),
        name=name,
    )(*scalars, *arrays)


def project_kernel(length_ref, *refs):
    row_refs, (mine_ref, other_ref, down, up_ref, out_ref, rows, weight, acc, row_sems, weight_sems) = refs[:-10], refs[-10:]
    c = lax.axis_index("c")
    row_copies = [pltpu.make_async_copy(row_refs[0], rows, row_sems.at[0])]
    for copy in row_copies:
        copy.start()
    z, x = lax.axis_index("z"), lax.axis_index("x")
    copies = [[] for _ in range(Z)]
    for j, dz in enumerate(RING):
        to_z = lax.rem(z + dz + Z, Z)
        for s, side in enumerate((mine_ref, other_ref)):
            for q, dx in enumerate(QUAD):
                to = (lax.rem(x + dx + X, X) * C + lax.rem(c + s, C)) * 64
                copies[j].append(
                    pltpu.make_async_copy(
                        side.at[pl.ds((q * Z + j) * 64, 64)],
                        weight.at[j, pl.ds(pl.multiple_of(to, 64), 64)],
                        weight_sems.at[j * 8 + s * 4 + q],
                    )
                )
                copies[j][-1].start()
    for copy in row_copies:
        copy.wait()
    low = jnp.zeros((512, 32), jnp.float32)
    for j, dz in enumerate(RING):
        to_z = lax.rem(z + dz + Z, Z)
        for copy in copies[j]:
            copy.wait()
        part = rows[:, pl.ds(pl.multiple_of(to_z * 512, 512), 512)]
        term = jnp.dot(part, weight[j], preferred_element_type=jnp.float32)
        if j == 0:
            acc[...] = term
        else:
            acc[...] += term
        low += lax.dot_general(part, down[to_z], (((1,), (1,)), ((), ())), preferred_element_type=jnp.float32)
    total = acc[...] + jnp.dot(low.astype(jnp.bfloat16), up_ref[...], preferred_element_type=jnp.float32)
    valid = lax.broadcasted_iota(jnp.int32, total.shape, 0) < length_ref[0]
    out_ref[...] = jnp.where(valid, total, 0.0).astype(jnp.bfloat16)


def per_device(
    prompts,
    layer_norm_gain,
    query_base_matrix,
    adapter_down_weight,
    adapter_up_weight,
    request_prompt_length,
    request_adapter_ident,
    adapter_pool_row,
):
    rows, noted, own = small(
        prepare_kernel,
        "prepare",
        (bf16(64, 4096), bf16(80, 512), bf16(2, 64, 512)),
        (request_adapter_ident, adapter_pool_row),
        prompts,
        layer_norm_gain.reshape(1, -1),
        query_base_matrix,
        adapter_down_weight,
        adapter_up_weight,
    )
    normed = (lax.all_gather(rows, "y", axis=0, tiled=True),)
    plane = to_all(own, "x", X).reshape(X * 2, 64, 512)
    trio = jnp.concatenate([shift(noted, dz=3), noted, shift(noted, dz=-3)], axis=0)
    plane, trio = lax.optimization_barrier((plane, trio))

    plane_other = swap(plane)
    ring = jnp.concatenate([trio, shift(trio, dz=1), shift(trio[:160], dz=-1)], axis=0)
    plane_other, ring = lax.optimization_barrier((plane_other, ring))
    ring = ring.reshape(Z, 80, 512)
    slots, weight = ring[:, 64, 0].astype(jnp.int32), ring[:, :64].reshape(512, 512)

    (wanted,) = small(pick_kernel, "pick", (bf16(Z, 64, 512),), (slots,), plane, plane_other)
    wanted, weight = lax.optimization_barrier((wanted, weight))
    planes = lax.all_to_all(wanted, "z", 0, 0)
    from_left, from_right = shift(weight, dx=1), shift(weight, dx=-1)
    core = lax.axis_index("c")
    far_pairs = [p for p in req_pairs(dx=1) if p[0] % C == 0] + [p for p in req_pairs(dx=-1) if p[0] % C == 1]
    planes, from_left, from_right = lax.optimization_barrier((planes, from_left, from_right))
    far = lax.ppermute(jnp.where(core == 0, from_left, from_right), REQ, far_pairs)

    adapter = lax.dynamic_index_in_dim(planes, slots[RING.index(0)] // (2 * X * C), 0, keepdims=False)
    spread = jnp.broadcast_to(adapter[:32], (Y, 32, 512))
    far, spread = lax.optimization_barrier((far, spread))
    down, up = lax.all_to_all(spread, "y", 0, 0), adapter[32:]
    mine = jnp.concatenate([weight, from_left, from_right, far], axis=0)
    other = swap(mine)

    any_space, vmem = pl.BlockSpec(memory_space=pl.ANY), pl.BlockSpec(memory_space=pltpu.VMEM)
    return pl.pallas_call(
        project_kernel,
        out_shape=bf16(512, 512),
        in_specs=[pl.BlockSpec(memory_space=pltpu.SMEM)] + [any_space] * (len(normed) + 2) + [vmem] * 2,
        out_specs=vmem,
        scratch_shapes=[
            pltpu.VMEM((512, 4096), jnp.bfloat16),
            pltpu.VMEM((8, 512, 512), jnp.bfloat16),
            pltpu.VMEM((512, 512), jnp.float32),
            pltpu.SemaphoreType.DMA((9,)),
            pltpu.SemaphoreType.DMA((64,)),
        ],
        compiler_params=pltpu.CompilerParams(vmem_limit_bytes=60 * 1024 * 1024),
        cost_estimate=pl.CostEstimate(flops=2 * 512 * 4096 * 544, bytes_accessed=9 << 20, transcendentals=0),
        name="project",
    )(request_prompt_length, *normed, mine, other, down, up)


def solution(mesh):
    mesh = jax.sharding.Mesh(mesh.devices.reshape(Z, X, C, Y), (*REQ, "y"))
    in_specs = (
        P((*REQ, "y"), None),
        P(),
        P(REQ, "y"),
        P(REQ, None, "y"),
        P(REQ, None, "y"),
        P(REQ),
        P(REQ),
        P(),
    )
    return jax.shard_map(
        per_device, mesh=mesh, in_specs=in_specs, out_specs=P(REQ, "y"), check_vma=False
    )
```

time: 346 us -> 134 us (0.39)
  waiting for transfers between devices: 276 us -> 35.3 us
  starting transfers between devices: 0.12 us -> 57.3 us
  blocking collectives: 24.1 us -> 0 us
  matrix products: 22.8 us -> 0 us
  Pallas kernels: 0 us -> 15.8 us
  other arithmetic: 8.11 us -> 1.89 us
  local copies, waits for them, and re-layouts: 0.2 us -> 5.51 us
    all_gather x4 -> x1, waiting for transfers between devices: 273 us -> 0.01 us  [per_device(): normed = (lax.all_gather(rows, 'y', axis=0, tiled=True),)]
    ppermute x0 -> x9, starting transfers between devices: none -> 41.3 us  [the longest x6 27.4 us: shift(): return lax.ppermute(value, REQ, req_pairs(**by))]
    psum x1 -> x0, blocking collectives: 24.1 us -> none  [per_device(): low = lax.psum(partial_value, 'tensor').astype(jnp.bfloat16)]
    ppermute x0 -> x9, waiting for transfers between devices: none -> 23.5 us  [the longest x6 21.8 us: shift(): return lax.ppermute(value, REQ, req_pairs(**by))]
    dot_general x5 -> x0, matrix products: 22.8 us -> none  [the longest x1 7.31 us: per_device(): jnp.einsum('qk,kcd->qcd', onehot, pieces[0], preferred_element_type=jnp.f...]
    all_to_all x0 -> x3, starting transfers between devices: none -> 16 us  [the longest x1 6.99 us: per_device(): down, up = (lax.all_to_all(spread, 'y', 0, 0), adapter[32:])]
    pallas_call x0 -> x3, Pallas kernels: none -> 15.8 us  [the longest x1 11.3 us: per_device(): pl.pallas_call(project_kernel, out_shape=bf16(512, 512), in_specs=[pl.Blo...]
    all_to_all x0 -> x3, waiting for transfers between devices: none -> 11.8 us  [the longest x1 11.7 us: per_device(): down, up = (lax.all_to_all(spread, 'y', 0, 0), adapter[32:])]
  transfers between devices with their start and end apart: 4 -> 13, of which waited for: 4 -> 8; matrix products, arithmetic and copies ran while one was open for 7% -> 5% of each run, Pallas kernels for 0% -> 2%
where the time goes in v2:
time: 134 us; the launch traced here: 133 us
  starting transfers between devices  57.3 us (43%)
  waiting for transfers between devices  35.3 us (26%)
  between operations  17.4 us (13%)
  Pallas kernels  15.8 us (12%)
  local copies, waits for them, and re-layouts  5.51 us (4%)
  other arithmetic  1.89 us (1%)
    ppermute x6, starting transfers between devices, shift(): return lax.ppermute(value, REQ, req_pairs(**by))  27.4 us
    ppermute x6, waiting for transfers between devices, shift(): return lax.ppermute(value, REQ, req_pairs(**by))  21.8 us
    all_to_all x1, waiting for transfers between devices, per_device(): down, up = (lax.all_to_all(spread, 'y', 0, 0), adapter[32:])  11.7 us
    pallas_call x1, Pallas kernels, per_device(): pl.pallas_call(project_kernel, out_shape=bf16(512, 512), in_specs=[pl.Blo...  11.3 us
    ppermute x2, starting transfers between devices, swap(): return lax.ppermute(value, 'c', [(0, 1), (1, 0)])  9.35 us
    all_to_all x1, starting transfers between devices, per_device(): down, up = (lax.all_to_all(spread, 'y', 0, 0), adapter[32:])  6.99 us
    all_to_all x1, starting transfers between devices, to_all(): lax.all_to_all(jnp.broadcast_to(value, (size, *value.shape)), axis, 0, 0)  4.84 us
    ppermute x1, starting transfers between devices, per_device(): lax.ppermute(jnp.where(core == 0, from_left, from_right), REQ, far_pairs)  4.58 us
  transfers between devices with their start and end apart: 13, of which 8 were waited for; matrix products, arithmetic and copies ran while one was open for 5% of the time, Pallas kernels for 2%

profile of v2, /device:TPU:1, one launch (start us, length us, event | category | flops | bytes accessed | tf_op | source)
XLA Modules:
  0.0 133.2 jit_solution(9614744628309556049)
XLA Ops:
  6.5 0.0 all-gather.2.cloned.1.call-start
  7.2 2.2 %prepare.1 = (bf16[64,4096]{1,0:T(8,128)(2,1)}, bf16[80,512]{1,0:T(8,128)(2,1)}, bf16[2,64,512]{2,1,0:T(8,128)(2,1)}) custom-call(s32[1]{0:T(128)S(6)} %copy.15.ident_ref, s32[128]{0:T(128)} %pool_ref.1, bf16[64,4096]{1,0:T(8,128)(2,1)} %rows_ref.1, f32[1,4096]{1,0:T(1,128)} %bitcast.18, bf16[64,512]{1,0:T(8,128)(2,1)} %base_ref.1, ...), custom_call_target="tpu_custom_call" | custom-call | bytes 2097152 | tf_op jit(solution)/shard_map/prepare/pallas_call | solution.py:76
  9.4 0.0 copy-start.4
  9.4 0.0 all-gather.2.cloned.1.call-update
  9.4 1.8 %broadcast_in_dim.6 = bf16[4,2,64,512]{3,2,1,0:T(8,128)(2,1)} broadcast(bf16[2,64,512]{2,1,0:T(8,128)(2,1)} %get-tuple-element.20), dimensions={1,2,3} | broadcast | bytes 655360 | tf_op jit(solution)/shard_map/broadcast_in_dim | solution.py:19
  11.2 4.8 %all-to-all-start = ((bf16[4,2,64,512]{3,2,1,0:T(8,128)(2,1)}), bf16[4,2,64,512]{3,2,1,0:T(8,128)(2,1)S(1)}, u32[]{:S(2)}, u32[]{:S(2)}) async-start(bf16[4,2,64,512]{3,2,1,0:T(8,128)(2,1)} %broadcast_in_dim.6), calls=%async_computation | async-start | bytes 1048576 | tf_op jit(solution)/shard_map/all_to_all | solution.py:19
  16.0 0.0 copy-done.4
  16.0 7.6 %collective-permute-start = (bf16[80,512]{1,0:T(8,128)(2,1)S(1)}, bf16[80,512]{1,0:T(8,128)(2,1)S(1)}, u32[]{:S(2)}, u32[]{:S(2)}) collective-permute-start(bf16[80,512]{1,0:T(8,128)(2,1)S(1)} %copy-done.4), channel_id=1, source_target_pairs={{0,192},{8,200},{16,208},{24,216},{32,224},{40,232},{48,240},{56,2... | collective-permute-start | bytes 245768 | tf_op jit(solution)/shard_map/ppermute | solution.py:32
  23.6 5.0 %collective-permute-start.1 = (bf16[80,512]{1,0:T(8,128)(2,1)S(1)}, bf16[80,512]{1,0:T(8,128)(2,1)S(1)}, u32[]{:S(2)}, u32[]{:S(2)}) collective-permute-start(bf16[80,512]{1,0:T(8,128)(2,1)S(1)} %copy-done.4), channel_id=1, source_target_pairs={{0,320},{8,328},{16,336},{24,344},{32,352},{40,360},{48,368},{56,3... | collective-permute-start | bytes 245768 | tf_op jit(solution)/shard_map/ppermute | solution.py:32
  28.6 0.1 collective-permute-done
  28.7 4.0 %collective-permute-done.1 = bf16[80,512]{1,0:T(8,128)(2,1)S(1)} collective-permute-done((bf16[80,512]{1,0:T(8,128)(2,1)S(1)}, bf16[80,512]{1,0:T(8,128)(2,1)S(1)}, u32[]{:S(2)}, u32[]{:S(2)}) %collective-permute-start.1) | collective-permute-done | bytes 81952 | tf_op jit(solution)/shard_map/ppermute | solution.py:32
  32.7 0.0 all-to-all-done
  32.7 0.0 copy-start.1
  32.7 4.1 %collective-permute-start.2 = (bf16[8,64,512]{2,1,0:T(8,128)(2,1)S(1)}, bf16[8,64,512]{2,1,0:T(8,128)(2,1)S(1)}, u32[]{:S(2)}, u32[]{:S(2)}) collective-permute-start(bf16[8,64,512]{2,1,0:T(8,128)(2,1)S(1)} %bitcast.13), channel_id=1, source_target_pairs={{0,8},{8,0},{1,9},{9,1},{2,10},{10,2},{3,11},{11,3},{4,12},{12,4},... | collective-permute-start | bytes 1572872 | tf_op jit(solution)/shard_map/ppermute | solution.py:40
  36.8 6.4 %collective-permute-start.3 = (bf16[240,512]{1,0:T(8,128)(2,1)S(1)}, bf16[240,512]{1,0:T(8,128)(2,1)S(1)}, u32[]{:S(2)}, u32[]{:S(2)}) collective-permute-start(bf16[240,512]{1,0:T(8,128)(2,1)S(1)} %pad_maximum_fusion.1), channel_id=1, source_target_pairs={{0,64},{8,72},{16,80},{24,88},{32,96},{40,104},{48,112},{56,120},{... | collective-permute-start | bytes 737288 | tf_op jit(solution)/shard_map/ppermute | solution.py:32
  43.2 1.9 %collective-permute-start.4 = (bf16[160,512]{1,0:T(8,128)(2,1)S(1)}, bf16[160,512]{1,0:T(8,128)(2,1)S(1)}, u32[]{:S(2)}, u32[]{:S(2)}) collective-permute-start(bf16[160,512]{1,0:T(8,128)(2,1)S(1)} %slice.25), channel_id=1, source_target_pairs={{0,448},{8,456},{16,464},{24,472},{32,480},{40,488},{48,496},{56,5... | collective-permute-start | bytes 491528 | tf_op jit(solution)/shard_map/ppermute | solution.py:32
  45.1 6.6 %collective-permute-done.4 = bf16[160,512]{1,0:T(8,128)(2,1)S(1)} collective-permute-done((bf16[160,512]{1,0:T(8,128)(2,1)S(1)}, bf16[160,512]{1,0:T(8,128)(2,1)S(1)}, u32[]{:S(2)}, u32[]{:S(2)}) %collective-permute-start.4) | collective-permute-done | bytes 163872 | tf_op jit(solution)/shard_map/ppermute | solution.py:32
  51.7 0.0 collective-permute-done.3
  51.7 0.0 collective-permute-done.2.other_ref
  51.7 0.0 copy-start.3
  51.8 0.1 copy.10
  51.9 0.6 fusion
  52.5 0.0 copy-done.1
  52.5 0.0 copy-done.3
  52.5 2.2 %pick.1 = bf16[8,64,512]{2,1,0:T(8,128)(2,1)} custom-call(s32[8]{0:T(128)} %get-tuple-element.38.slots_ref, bf16[8,64,512]{2,1,0:T(8,128)(2,1)} %bitcast.14, bf16[8,64,512]{2,1,0:T(8,128)(2,1)} %copy-done.3), custom_call_target="tpu_custom_call" | custom-call | bytes 2097152 | tf_op jit(solution)/shard_map/pick/pallas_call | solution.py:76
  54.8 4.2 %all-to-all-start.1 = ((bf16[8,64,512]{2,1,0:T(8,128)(2,1)}), bf16[8,64,512]{2,1,0:T(8,128)(2,1)}, u32[]{:S(2)}, u32[]{:S(2)}) async-start(bf16[8,64,512]{2,1,0:T(8,128)(2,1)} %pick.1), calls=%async_computation.1 | async-start | bytes 1048576 | tf_op jit(solution)/shard_map/all_to_all | solution.py:160
  58.9 3.4 %collective-permute-start.5 = (bf16[512,512]{1,0:T(8,128)(2,1)S(1)}, bf16[512,512]{1,0:T(8,128)(2,1)S(1)}, u32[]{:S(2)}, u32[]{:S(2)}) collective-permute-start(bf16[512,512]{1,0:T(8,128)(2,1)S(1)} %bitcast.15), channel_id=1, source_target_pairs={{0,16},{8,24},{16,32},{24,40},{32,48},{40,56},{48,0},{56,8},{64,80... | collective-permute-start | bytes 1572872 | tf_op jit(solution)/shard_map/ppermute | solution.py:32
  62.3 3.1 %collective-permute-start.6 = (bf16[512,512]{1,0:T(8,128)(2,1)S(1)}, bf16[512,512]{1,0:T(8,128)(2,1)}, u32[]{:S(2)}, u32[]{:S(2)}) collective-permute-start(bf16[512,512]{1,0:T(8,128)(2,1)S(1)} %bitcast.16), channel_id=1, source_target_pairs={{0,48},{8,56},{16,0},{24,8},{32,16},{40,24},{48,32},{56,40},{64,11... | collective-permute-start | bytes 1572872 | tf_op jit(solution)/shard_map/ppermute | solution.py:32
  65.5 9.4 %collective-permute-done.5 = bf16[512,512]{1,0:T(8,128)(2,1)S(1)} collective-permute-done((bf16[512,512]{1,0:T(8,128)(2,1)S(1)}, bf16[512,512]{1,0:T(8,128)(2,1)S(1)}, u32[]{:S(2)}, u32[]{:S(2)}) %collective-permute-start.5) | collective-permute-done | bytes 524320 | tf_op jit(solution)/shard_map/ppermute | solution.py:32
  74.9 1.8 %collective-permute-done.6 = bf16[512,512]{1,0:T(8,128)(2,1)} collective-permute-done((bf16[512,512]{1,0:T(8,128)(2,1)S(1)}, bf16[512,512]{1,0:T(8,128)(2,1)}, u32[]{:S(2)}, u32[]{:S(2)}) %collective-permute-start.6) | collective-permute-done | bytes 524320 | tf_op jit(solution)/shard_map/ppermute | solution.py:32
  76.8 0.1 all-to-all-done.1
  76.9 1.2 broadcast_select_fusion
  78.1 4.6 %collective-permute-start.7 = (bf16[512,512]{1,0:T(8,128)(2,1)S(1)}, bf16[512,512]{1,0:T(8,128)(2,1)S(1)}, u32[]{:S(2)}, u32[]{:S(2)}) collective-permute-start(bf16[512,512]{1,0:T(8,128)(2,1)S(1)} %get-tuple-element.35), channel_id=1, source_target_pairs={{0,16},{16,32},{32,48},{48,0},{64,80},{80,96},{96,112},{112,64},{1... | collective-permute-start | bytes 1572872 | tf_op jit(solution)/shard_map/ppermute | solution.py:165
  82.7 0.6 slice.28
  85.8 1.4 %dynamic-slice_bitcast_fusion = (bf16[32,512]{1,0:T(8,128)(2,1)}, bf16[32,512]{1,0:T(8,128)(2,1)S(1)}) fusion(bf16[8,64,512]{2,1,0:T(8,128)(2,1)} %all-to-all-done.1, s32[]{:T(128)S(6)} %select_n.20, s32[]{:T(128)S(6)} %add.6), kind=kLoop, calls=%fused_computation.3 | loop fusion | bytes 131080 | tf_op jit(solution)/shard_map/slice | solution.py:170
  87.2 1.6 %collective-permute-done.7 = bf16[512,512]{1,0:T(8,128)(2,1)S(1)} collective-permute-done((bf16[512,512]{1,0:T(8,128)(2,1)S(1)}, bf16[512,512]{1,0:T(8,128)(2,1)S(1)}, u32[]{:S(2)}, u32[]{:S(2)}) %collective-permute-start.7) | collective-permute-done | bytes 524320 | tf_op jit(solution)/shard_map/ppermute | solution.py:165
  88.8 0.7 broadcast_in_dim.7
  89.6 0.0 copy-start
  89.6 5.3 %collective-permute-start.8 = (bf16[2048,512]{1,0:T(8,128)(2,1)S(1)}, bf16[2048,512]{1,0:T(8,128)(2,1)}, u32[]{:S(2)}, u32[]{:S(2)}) collective-permute-start(bf16[2048,512]{1,0:T(8,128)(2,1)S(1)} %constant_dynamic-update-slice_fusion.refs_1_), channel_id=1, source_target_pairs={{0,8},{8,0},{1,9},{9,1},{2,10},{10,2},{3,11},{11,3},{4,12},{12,4},... | collective-permute-start | bytes 6291464 | tf_op jit(solution)/shard_map/ppermute | solution.py:40
  94.9 7.0 %all-to-all-start.2 = ((bf16[8,32,512]{2,1,0:T(8,128)(2,1)}), bf16[8,32,512]{2,1,0:T(8,128)(2,1)S(1)}, u32[]{:S(2)}, u32[]{:S(2)}) async-start(bf16[8,32,512]{2,1,0:T(8,128)(2,1)} %broadcast_in_dim.7), calls=%async_computation.2 | async-start | bytes 524288 | tf_op jit(solution)/shard_map/all_to_all | solution.py:170
  102.5 11.7 %all-to-all-done.2.refs_3_ = bf16[8,32,512]{2,1,0:T(8,128)(2,1)S(1)} async-done(((bf16[8,32,512]{2,1,0:T(8,128)(2,1)}), bf16[8,32,512]{2,1,0:T(8,128)(2,1)S(1)}, u32[]{:S(2)}, u32[]{:S(2)}) %all-to-all-start.2) | async-done | bytes 262176 | tf_op jit(solution)/shard_map/all_to_all | solution.py:170
  114.2 0.0 copy-start.2
  114.2 0.0 collective-permute-done.8.refs_2_
  114.2 0.0 all-gather.2.cloned.1.call-done.refs_0_
  114.3 0.0 copy-done
  114.3 0.7 copy-done.2
  115.0 11.3 %project.1 = bf16[512,512]{1,0:T(8,128)(2,1)} custom-call(s32[1]{0:T(128)S(6)} %copy.14.length_ref, bf16[512,4096]{1,0:T(8,128)(2,1)} %all-gather.2.cloned.1.call-done.refs_0_, bf16[2048,512]{1,0:T(8,128)(2,1)} %copy-done, bf16[2048,512]{1,0:T(8,128)(2,1)} %collective-permute-done.8.refs_2_, bf16[8,32,512]{2,1,0:T(8,128)(2,1)} %copy-done.2, ...), custom_call_target="tpu_custom_call" | custom-call | flops 2281701376 | bytes 9437184 | tf_op jit(solution)/shard_map/project/pallas_call | solution.py:175
  (8 shorter events, 0.2 us)
Async XLA Ops:
  6.5 107.7 %all-gather.2.cloned.1.call-start = ((), (), s32[]{:S(2)}) async-start(), calls=%async_computation.3 | async-start | bytes 4718592 | tf_op jit(solution)/shard_map/all_gather | solution.py:147
  9.4 6.7 %copy-start.4 = (bf16[80,512]{1,0:T(8,128)(2,1)S(1)}, bf16[80,512]{1,0:T(8,128)(2,1)}, u32[]{:S(2)}) copy-start(bf16[80,512]{1,0:T(8,128)(2,1)} %get-tuple-element.21) | copy-start | bytes 245764
  11.2 21.5 %all-to-all-start = ((bf16[4,2,64,512]{3,2,1,0:T(8,128)(2,1)}), bf16[4,2,64,512]{3,2,1,0:T(8,128)(2,1)S(1)}, u32[]{:S(2)}, u32[]{:S(2)}) async-start(bf16[4,2,64,512]{3,2,1,0:T(8,128)(2,1)} %broadcast_in_dim.6), calls=%async_computation | async-start | bytes 1048576 | tf_op jit(solution)/shard_map/all_to_all | solution.py:19
  16.0 12.7 %collective-permute-start = (bf16[80,512]{1,0:T(8,128)(2,1)S(1)}, bf16[80,512]{1,0:T(8,128)(2,1)S(1)}, u32[]{:S(2)}, u32[]{:S(2)}) collective-permute-start(bf16[80,512]{1,0:T(8,128)(2,1)S(1)} %copy-done.4), channel_id=1, source_target_pairs={{0,192},{8,200},{16,208},{24,216},{32,224},{40,232},{48,240},{56,2... | collective-permute-start | bytes 245768 | tf_op jit(solution)/shard_map/ppermute | solution.py:32
  23.6 9.0 %collective-permute-start.1 = (bf16[80,512]{1,0:T(8,128)(2,1)S(1)}, bf16[80,512]{1,0:T(8,128)(2,1)S(1)}, u32[]{:S(2)}, u32[]{:S(2)}) collective-permute-start(bf16[80,512]{1,0:T(8,128)(2,1)S(1)} %copy-done.4), channel_id=1, source_target_pairs={{0,320},{8,328},{16,336},{24,344},{32,352},{40,360},{48,368},{56,3... | collective-permute-start | bytes 245768 | tf_op jit(solution)/shard_map/ppermute | solution.py:32
  32.7 19.9 %copy-start.1 = (bf16[4,2,64,512]{3,2,1,0:T(8,128)(2,1)}, bf16[4,2,64,512]{3,2,1,0:T(8,128)(2,1)S(1)}, u32[]{:S(2)}) copy-start(bf16[4,2,64,512]{3,2,1,0:T(8,128)(2,1)S(1)} %all-to-all-done) | copy-start | bytes 1572868
  32.7 19.0 %collective-permute-start.2 = (bf16[8,64,512]{2,1,0:T(8,128)(2,1)S(1)}, bf16[8,64,512]{2,1,0:T(8,128)(2,1)S(1)}, u32[]{:S(2)}, u32[]{:S(2)}) collective-permute-start(bf16[8,64,512]{2,1,0:T(8,128)(2,1)S(1)} %bitcast.13), channel_id=1, source_target_pairs={{0,8},{8,0},{1,9},{9,1},{2,10},{10,2},{3,11},{11,3},{4,12},{12,4},... | collective-permute-start | bytes 1572872 | tf_op jit(solution)/shard_map/ppermute | solution.py:40
  36.8 14.9 %collective-permute-start.3 = (bf16[240,512]{1,0:T(8,128)(2,1)S(1)}, bf16[240,512]{1,0:T(8,128)(2,1)S(1)}, u32[]{:S(2)}, u32[]{:S(2)}) collective-permute-start(bf16[240,512]{1,0:T(8,128)(2,1)S(1)} %pad_maximum_fusion.1), channel_id=1, source_target_pairs={{0,64},{8,72},{16,80},{24,88},{32,96},{40,104},{48,112},{56,120},{... | collective-permute-start | bytes 737288 | tf_op jit(solution)/shard_map/ppermute | solution.py:32
  43.2 8.5 %collective-permute-start.4 = (bf16[160,512]{1,0:T(8,128)(2,1)S(1)}, bf16[160,512]{1,0:T(8,128)(2,1)S(1)}, u32[]{:S(2)}, u32[]{:S(2)}) collective-permute-start(bf16[160,512]{1,0:T(8,128)(2,1)S(1)} %slice.25), channel_id=1, source_target_pairs={{0,448},{8,456},{16,464},{24,472},{32,480},{40,488},{48,496},{56,5... | collective-permute-start | bytes 491528 | tf_op jit(solution)/shard_map/ppermute | solution.py:32
  51.7 0.8 copy-start.3
  54.8 22.1 %all-to-all-start.1 = ((bf16[8,64,512]{2,1,0:T(8,128)(2,1)}), bf16[8,64,512]{2,1,0:T(8,128)(2,1)}, u32[]{:S(2)}, u32[]{:S(2)}) async-start(bf16[8,64,512]{2,1,0:T(8,128)(2,1)} %pick.1), calls=%async_computation.1 | async-start | bytes 1048576 | tf_op jit(solution)/shard_map/all_to_all | solution.py:160
  58.9 16.0 %collective-permute-start.5 = (bf16[512,512]{1,0:T(8,128)(2,1)S(1)}, bf16[512,512]{1,0:T(8,128)(2,1)S(1)}, u32[]{:S(2)}, u32[]{:S(2)}) collective-permute-start(bf16[512,512]{1,0:T(8,128)(2,1)S(1)} %bitcast.15), channel_id=1, source_target_pairs={{0,16},{8,24},{16,32},{24,40},{32,48},{40,56},{48,0},{56,8},{64,80... | collective-permute-start | bytes 1572872 | tf_op jit(solution)/shard_map/ppermute | solution.py:32
  62.3 14.4 %collective-permute-start.6 = (bf16[512,512]{1,0:T(8,128)(2,1)S(1)}, bf16[512,512]{1,0:T(8,128)(2,1)}, u32[]{:S(2)}, u32[]{:S(2)}) collective-permute-start(bf16[512,512]{1,0:T(8,128)(2,1)S(1)} %bitcast.16), channel_id=1, source_target_pairs={{0,48},{8,56},{16,0},{24,8},{32,16},{40,24},{48,32},{56,40},{64,11... | collective-permute-start | bytes 1572872 | tf_op jit(solution)/shard_map/ppermute | solution.py:32
  78.1 10.7 %collective-permute-start.7 = (bf16[512,512]{1,0:T(8,128)(2,1)S(1)}, bf16[512,512]{1,0:T(8,128)(2,1)S(1)}, u32[]{:S(2)}, u32[]{:S(2)}) collective-permute-start(bf16[512,512]{1,0:T(8,128)(2,1)S(1)} %get-tuple-element.35), channel_id=1, source_target_pairs={{0,16},{16,32},{32,48},{48,0},{64,80},{80,96},{96,112},{112,64},{1... | collective-permute-start | bytes 1572872 | tf_op jit(solution)/shard_map/ppermute | solution.py:165
  89.6 24.7 %copy-start = (bf16[2048,512]{1,0:T(8,128)(2,1)}, bf16[2048,512]{1,0:T(8,128)(2,1)S(1)}, u32[]{:S(2)}) copy-start(bf16[2048,512]{1,0:T(8,128)(2,1)S(1)} %constant_dynamic-update-slice_fusion.refs_1_) | copy-start | bytes 6291460
  89.6 24.6 %collective-permute-start.8 = (bf16[2048,512]{1,0:T(8,128)(2,1)S(1)}, bf16[2048,512]{1,0:T(8,128)(2,1)}, u32[]{:S(2)}, u32[]{:S(2)}) collective-permute-start(bf16[2048,512]{1,0:T(8,128)(2,1)S(1)} %constant_dynamic-update-slice_fusion.refs_1_), channel_id=1, source_target_pairs={{0,8},{8,0},{1,9},{9,1},{2,10},{10,2},{3,11},{11,3},{4,12},{12,4},... | collective-permute-start | bytes 6291464 | tf_op jit(solution)/shard_map/ppermute | solution.py:40
  94.9 19.4 %all-to-all-start.2 = ((bf16[8,32,512]{2,1,0:T(8,128)(2,1)}), bf16[8,32,512]{2,1,0:T(8,128)(2,1)S(1)}, u32[]{:S(2)}, u32[]{:S(2)}) async-start(bf16[8,32,512]{2,1,0:T(8,128)(2,1)} %broadcast_in_dim.7), calls=%async_computation.2 | async-start | bytes 524288 | tf_op jit(solution)/shard_map/all_to_all | solution.py:170
  114.2 0.7 copy-start.2
Sparse Core Ops, SparseCore 0:
  9.5 62.6 all-gather.1

commit v3 on v2

v3 whole, which is shorter than its diff:
```python
import jax
import jax.numpy as jnp
from jax import lax
from jax.experimental import pallas as pl
from jax.experimental.pallas import tpu as pltpu
from jax.sharding import PartitionSpec as P

QUAD = (0, -1, 1, 2)
Z, X, C, Y = 8, 4, 2, 8
REQ = ("z", "x", "c")


def after(value, *others):
    return lax.optimization_barrier((value, *others))[0]


def to_all(value, axis, size):
    return lax.all_to_all(jnp.broadcast_to(value, (size, *value.shape)), axis, 0, 0)


def req_pairs(dz=0, dx=0):
    return [
        ((z * X + x) * C + c, (((z + dz) % Z) * X + (x + dx) % X) * C + c)
        for z in range(Z)
        for x in range(X)
        for c in range(C)
    ]


def shift(value, **by):
    return lax.ppermute(value, REQ, req_pairs(**by))


def shift_y(value, by):
    return lax.ppermute(value, "y", [(y, (y + by) % Y) for y in range(Y)])


def swap(value):
    return lax.ppermute(value, "c", [(0, 1), (1, 0)])


def prepare_kernel(ident_ref, pool_ref, rows_ref, gain_ref, weight_ref, down_ref, up_ref, rows_out, weight_out, pair_out):
    slot = jnp.full((16, 512), pool_ref[ident_ref[0]].astype(jnp.float32)).astype(jnp.bfloat16)
    for z in range(Z):
        weight_out[z, :64] = weight_ref[...]
        weight_out[z, 64:] = slot
    values = rows_ref[...].astype(jnp.float32)
    scale = lax.rsqrt(jnp.mean(values * values, axis=-1, keepdims=True) + 1e-06)
    rows_out[...] = (values * scale * gain_ref[...]).astype(jnp.bfloat16)
    pair_out[:, :32] = down_ref[...]
    pair_out[:, 32:] = up_ref[...]


def pick_kernel(slots_ref, mine_ref, other_ref, out_ref):
    x, c = lax.axis_index("x"), lax.axis_index("c")
    for to in range(Z):
        slot = slots_ref[to]
        owner = lax.rem(lax.div(slot, 2), X * C)
        dx = lax.rem(lax.div(owner, C) - x + X, X)
        block = jnp.where(dx == 0, 0, jnp.where(dx == 3, 1, jnp.where(dx == 1, 2, 3)))
        at = block * 2 + lax.rem(slot, 2)

        @pl.when(lax.rem(owner, C) == c)
        def _(to=to, at=at):
            out_ref[to] = mine_ref[at]

        @pl.when(lax.rem(owner, C) != c)
        def _(to=to, at=at):
            out_ref[to] = other_ref[at]


def bf16(*shape):
    return jax.ShapeDtypeStruct(shape, jnp.bfloat16)


def small(kernel, name, out_shape, scalars, *arrays):
    smem, vmem = pl.BlockSpec(memory_space=pltpu.SMEM), pl.BlockSpec(memory_space=pltpu.VMEM)
    return pl.pallas_call(
        kernel,
        out_shape=out_shape,
        in_specs=[smem] * len(scalars) + [vmem] * len(arrays),
        out_specs=[vmem] * len(out_shape),
        cost_estimate=pl.CostEstimate(flops=0, bytes_accessed=2 << 20, transcendentals=0),
        name=name,
    )(*scalars, *arrays)


def base_kernel(rows_ref, mine_ref, mine_close_ref, mine_far_ref, other_ref, other_close_ref, other_far_ref, out_ref, rows, weight, row_sems, weight_sems):
    x, c = lax.axis_index("x"), lax.axis_index("c")
    copies = []
    for j in range(Z):
        here = [pltpu.make_async_copy(rows_ref.at[:, pl.ds(j * 512, 512)], rows.at[j], row_sems.at[j])]
        sides = ((mine_ref, mine_close_ref, mine_far_ref), (other_ref, other_close_ref, other_far_ref))
        for s, (here_ref, close_ref, far_ref) in enumerate(sides):
            for q, dx in enumerate(QUAD):
                to = (lax.rem(x + dx + X, X) * C + lax.rem(c + s, C)) * 64
                here.append(
                    pltpu.make_async_copy(
                        (here_ref, close_ref, close_ref, far_ref)[q].at[pl.ds(((q == 2) * Z + j) * 64, 64)],
                        weight.at[j, pl.ds(pl.multiple_of(to, 64), 64)],
                        weight_sems.at[j * 8 + s * 4 + q],
                    )
                )
        for copy in here:
            copy.start()
        copies.append(here)
    for j in range(Z):
        for copy in copies[j]:
            copy.wait()
        term = jnp.dot(rows[j], weight[j], preferred_element_type=jnp.float32)
        if j == 0:
            out_ref[...] = term
        else:
            out_ref[...] += term


def adapt_kernel(length_ref, rows_ref, base_ref, adapters, out_ref, rows, row_sems):
    copies = [
        pltpu.make_async_copy(rows_ref.at[:, pl.ds(y * 512, 512)], rows.at[y], row_sems.at[y]) for y in range(Y)
    ]
    for copy in copies:
        copy.start()
    low = jnp.zeros((32, 512), jnp.float32)
    for y in range(Y):
        copies[y].wait()
        low += lax.dot_general(adapters[y, :32], rows[y], (((1,), (1,)), ((), ())), preferred_element_type=jnp.float32)
    low = low.astype(jnp.bfloat16)
    total = base_ref[...] + lax.dot_general(
        low, adapters[lax.axis_index("y"), 32:], (((0,), (0,)), ((), ())), preferred_element_type=jnp.float32
    )
    valid = lax.broadcasted_iota(jnp.int32, total.shape, 0) < length_ref[0]
    out_ref[...] = jnp.where(valid, total, 0.0).astype(jnp.bfloat16)


def per_device(
    prompts,
    layer_norm_gain,
    query_base_matrix,
    adapter_down_weight,
    adapter_up_weight,
    request_prompt_length,
    request_adapter_ident,
    adapter_pool_row,
):
    rows, noted, own = small(
        prepare_kernel,
        "prepare",
        (bf16(64, 4096), bf16(Z, 80, 512), bf16(2, 64, 512)),
        (request_adapter_ident, adapter_pool_row),
        prompts,
        layer_norm_gain.reshape(1, -1),
        query_base_matrix,
        adapter_down_weight,
        adapter_up_weight,
    )
    normed = lax.all_gather(rows, "y", axis=0, tiled=True)
    ring = lax.all_to_all(noted, "z", 0, 0)
    plane = jnp.concatenate([own, shift(own, dx=1), shift(own, dx=-1), shift(own, dx=2)], axis=0)
    plane_other = swap(plane)
    slots, weight = ring[:, 64, 0].astype(jnp.int32), ring[:, :64].reshape(512, 512)
    (wanted,) = small(pick_kernel, "pick", (bf16(Z, 64, 512),), (slots,), plane, plane_other)

    planes = lax.all_to_all(wanted, "z", 0, 0)
    weight_other = swap(after(weight, wanted))
    weight = after(weight, weight_other)
    from_left, from_right = shift(weight, dx=1), shift(weight, dx=-1)
    core = lax.axis_index("c")
    far_pairs = [p for p in req_pairs(dx=1) if p[0] % C == 0] + [p for p in req_pairs(dx=-1) if p[0] % C == 1]
    adapter = lax.dynamic_index_in_dim(planes, slots[lax.axis_index("z")] // (2 * X * C), 0, keepdims=False)
    spread = jnp.broadcast_to(adapter, (Y, 64, 512))
    adapters = lax.all_to_all(spread, "y", 0, 0)
    far = lax.ppermute(after(jnp.where(core == 0, from_left, from_right), spread), REQ, far_pairs)
    close = jnp.concatenate([from_left, from_right], axis=0)
    sides = ((weight, close, far), (weight_other, swap(close), swap(far)))

    any_space, vmem = pl.BlockSpec(memory_space=pl.ANY), pl.BlockSpec(memory_space=pltpu.VMEM)
    total = pl.pallas_call(
        base_kernel,
        out_shape=jax.ShapeDtypeStruct((512, 512), jnp.float32),
        in_specs=[any_space] * 7,
        out_specs=vmem,
        scratch_shapes=[
            pltpu.VMEM((8, 512, 512), jnp.bfloat16),
            pltpu.VMEM((8, 512, 512), jnp.bfloat16),
            pltpu.SemaphoreType.DMA((8,)),
            pltpu.SemaphoreType.DMA((64,)),
        ],
        compiler_params=pltpu.CompilerParams(vmem_limit_bytes=60 * 1024 * 1024),
        cost_estimate=pl.CostEstimate(flops=2 * 512 * 4096 * 512, bytes_accessed=9 << 20, transcendentals=0),
        name="base",
    )(normed, *sides[0], *sides[1])
    return pl.pallas_call(
        adapt_kernel,
        out_shape=bf16(512, 512),
        in_specs=[pl.BlockSpec(memory_space=pltpu.SMEM), any_space] + [vmem] * 2,
        out_specs=vmem,
        scratch_shapes=[pltpu.VMEM((8, 512, 512), jnp.bfloat16), pltpu.SemaphoreType.DMA((8,))],
        compiler_params=pltpu.CompilerParams(vmem_limit_bytes=60 * 1024 * 1024),
        cost_estimate=pl.CostEstimate(flops=2 * 512 * 4096 * 32, bytes_accessed=6 << 20, transcendentals=0),
        name="adapt",
    )(request_prompt_length, normed, total, adapters)


def solution(mesh):
    mesh = jax.sharding.Mesh(mesh.devices.reshape(Z, X, C, Y), (*REQ, "y"))
    in_specs = (
        P((*REQ, "y"), None),
        P(),
        P(REQ, "y"),
        P(REQ, None, "y"),
        P(REQ, None, "y"),
        P(REQ),
        P(REQ),
        P(),
    )
    return jax.shard_map(
        per_device, mesh=mesh, in_specs=in_specs, out_specs=P(REQ, "y"), check_vma=False
    )
```

time: 134 us -> 117 us (0.87)
  waiting for transfers between devices: 35.3 us -> 20.8 us
  starting transfers between devices: 57.3 us -> 54.9 us
    ppermute x6 -> x5, waiting for transfers between devices: 21.8 us -> 3.31 us  [shift(): return lax.ppermute(value, REQ, req_pairs(**by))]
    ppermute x6 -> x5, starting transfers between devices: 27.4 us -> 16.4 us  [shift(): return lax.ppermute(value, REQ, req_pairs(**by))]
    all_to_all x1, waiting for transfers between devices: 0.13 us -> 8.28 us  [per_device(): planes = lax.all_to_all(wanted, 'z', 0, 0)]
    all_to_all x2, starting transfers between devices: 11.8 us -> 17.6 us  [the longest x1 10.9 us: per_device(): ring = lax.all_to_all(noted, 'z', 0, 0)]
    all_to_all x2, waiting for transfers between devices: 11.7 us -> 7.94 us  [the longest x1 5.69 us: per_device(): adapters = lax.all_to_all(spread, 'y', 0, 0)]
    unnamed x13 -> x16, local copies, waits for them, and re-layouts: 0.89 us -> 3.56 us
    slice x4 -> x0, local copies, waits for them, and re-layouts: 2.04 us -> none  [the longest x1 1.4 us: per_device(): down, up = (lax.all_to_all(spread, 'y', 0, 0), adapter[32:])]
    ppermute x2 -> x4, starting transfers between devices: 9.35 us -> 11.2 us  [swap(): return lax.ppermute(value, 'c', [(0, 1), (1, 0)])]
  transfers between devices with their start and end apart: 13 -> 14, of which waited for: 8 -> 5; matrix products, arithmetic and copies ran while one was open for 5% -> 4% of each run, Pallas kernels for 2% -> 8%
where the time goes in v3:
time: 117 us; the launch traced here: 116 us
  starting transfers between devices  54.9 us (47%)
  waiting for transfers between devices  20.8 us (18%)
  between operations  17.5 us (15%)
  Pallas kernels  16.4 us (14%)
  local copies, waits for them, and re-layouts  5.14 us (4%)
  other arithmetic  1.8 us (2%)
    ppermute x5, starting transfers between devices, shift(): return lax.ppermute(value, REQ, req_pairs(**by))  16.4 us
    ppermute x4, starting transfers between devices, swap(): return lax.ppermute(value, 'c', [(0, 1), (1, 0)])  11.2 us
    all_to_all x1, starting transfers between devices, per_device(): ring = lax.all_to_all(noted, 'z', 0, 0)  10.9 us
    all_to_all x1, waiting for transfers between devices, per_device(): planes = lax.all_to_all(wanted, 'z', 0, 0)  8.28 us
    all_to_all x1, starting transfers between devices, per_device(): adapters = lax.all_to_all(spread, 'y', 0, 0)  6.74 us
    pallas_call x1, Pallas kernels, per_device(): pl.pallas_call(base_kernel, out_shape=jax.ShapeDtypeStruct((512, 512), jn...  6.72 us
    all_to_all x1, waiting for transfers between devices, per_device(): adapters = lax.all_to_all(spread, 'y', 0, 0)  5.69 us
    all_to_all x1, starting transfers between devices, per_device(): planes = lax.all_to_all(wanted, 'z', 0, 0)  5.19 us
  transfers between devices with their start and end apart: 14, of which 5 were waited for; matrix products, arithmetic and copies ran while one was open for 4% of the time, Pallas kernels for 8%

profile of v3, /device:TPU:1, one launch (start us, length us, event | category | flops | bytes accessed | tf_op | source)
XLA Modules:
  0.0 116.5 jit_solution(13721315367983834077)
XLA Ops:
  6.5 0.0 all-gather.2.cloned.1.call-start
  7.2 2.3 %prepare.1 = (bf16[64,4096]{1,0:T(8,128)(2,1)}, bf16[8,80,512]{2,1,0:T(8,128)(2,1)}, bf16[2,64,512]{2,1,0:T(8,128)(2,1)}) custom-call(s32[1]{0:T(128)S(6)} %copy.14.ident_ref, s32[128]{0:T(128)} %pool_ref.1, bf16[64,4096]{1,0:T(8,128)(2,1)} %rows_ref.1, f32[1,4096]{1,0:T(1,128)} %bitcast.9, bf16[64,512]{1,0:T(8,128)(2,1)} %weight_ref.1, ...), custom_call_target="tpu_custom_call" | custom-call | bytes 2097152 | tf_op jit(solution)/shard_map/prepare/pallas_call | solution.py:78
  9.5 0.0 all-gather.2.cloned.1.call-update
  9.5 10.9 %all-to-all-start = ((bf16[8,80,512]{2,1,0:T(8,128)(2,1)}), bf16[8,80,512]{2,1,0:T(8,128)(2,1)S(1)}, u32[]{:S(2)}, u32[]{:S(2)}) async-start(bf16[8,80,512]{2,1,0:T(8,128)(2,1)} %get-tuple-element.12), calls=%async_computation | async-start | bytes 1310720 | tf_op jit(solution)/shard_map/all_to_all | solution.py:157
  20.4 3.1 %collective-permute-start = (bf16[2,64,512]{2,1,0:T(8,128)(2,1)}, bf16[2,64,512]{2,1,0:T(8,128)(2,1)S(1)}, u32[]{:S(2)}, u32[]{:S(2)}) collective-permute-start(bf16[2,64,512]{2,1,0:T(8,128)(2,1)} %get-tuple-element.13), channel_id=1, source_target_pairs={{0,16},{8,24},{16,32},{24,40},{32,48},{40,56},{48,0},{56,8},{64,80... | collective-permute-start | bytes 393224 | tf_op jit(solution)/shard_map/ppermute | solution.py:31
  23.5 3.4 %collective-permute-start.1 = (bf16[2,64,512]{2,1,0:T(8,128)(2,1)}, bf16[2,64,512]{2,1,0:T(8,128)(2,1)S(1)}, u32[]{:S(2)}, u32[]{:S(2)}) collective-permute-start(bf16[2,64,512]{2,1,0:T(8,128)(2,1)} %get-tuple-element.13), channel_id=1, source_target_pairs={{0,48},{8,56},{16,0},{24,8},{32,16},{40,24},{48,32},{56,40},{64,11... | collective-permute-start | bytes 393224 | tf_op jit(solution)/shard_map/ppermute | solution.py:31
  26.9 3.4 %collective-permute-start.2 = (bf16[2,64,512]{2,1,0:T(8,128)(2,1)}, bf16[2,64,512]{2,1,0:T(8,128)(2,1)S(1)}, u32[]{:S(2)}, u32[]{:S(2)}) collective-permute-start(bf16[2,64,512]{2,1,0:T(8,128)(2,1)} %get-tuple-element.13), channel_id=1, source_target_pairs={{0,32},{8,40},{16,48},{24,56},{32,0},{40,8},{48,16},{56,24},{64,96... | collective-permute-start | bytes 393224 | tf_op jit(solution)/shard_map/ppermute | solution.py:31
  30.4 0.9 constant_dynamic-update-slice_fusion.3
  31.3 0.0 collective-permute-done
  31.3 0.0 collective-permute-done.1
  31.3 3.3 %collective-permute-done.2 = bf16[2,64,512]{2,1,0:T(8,128)(2,1)S(1)} collective-permute-done((bf16[2,64,512]{2,1,0:T(8,128)(2,1)}, bf16[2,64,512]{2,1,0:T(8,128)(2,1)S(1)}, u32[]{:S(2)}, u32[]{:S(2)}) %collective-permute-start.2) | collective-permute-done | bytes 131104 | tf_op jit(solution)/shard_map/ppermute | solution.py:31
  34.7 0.0 copy-start.4
  34.7 4.3 %collective-permute-start.3 = (bf16[8,64,512]{2,1,0:T(8,128)(2,1)S(1)}, bf16[8,64,512]{2,1,0:T(8,128)(2,1)S(1)}, u32[]{:S(2)}, u32[]{:S(2)}) collective-permute-start(bf16[8,64,512]{2,1,0:T(8,128)(2,1)S(1)} %constant_dynamic-update-slice_fusion.mine_ref), channel_id=1, source_target_pairs={{0,8},{8,0},{1,9},{9,1},{2,10},{10,2},{3,11},{11,3},{4,12},{12,4},... | collective-permute-start | bytes 1572872 | tf_op jit(solution)/shard_map/ppermute | solution.py:39
  38.9 2.3 %all-to-all-done = bf16[8,80,512]{2,1,0:T(8,128)(2,1)S(1)} async-done(((bf16[8,80,512]{2,1,0:T(8,128)(2,1)}), bf16[8,80,512]{2,1,0:T(8,128)(2,1)S(1)}, u32[]{:S(2)}, u32[]{:S(2)}) %all-to-all-start) | async-done | bytes 655392 | tf_op jit(solution)/shard_map/all_to_all | solution.py:157
  41.2 0.0 copy-start.1
  41.2 0.8 fusion.slots_ref
  42.1 0.0 collective-permute-done.3.other_ref
  42.1 0.0 copy-done.4
  42.1 0.0 copy-start.5
  42.1 0.8 copy-done.5
  42.9 2.3 %pick.1 = bf16[8,64,512]{2,1,0:T(8,128)(2,1)} custom-call(s32[8]{0:T(128)} %fusion.slots_ref, bf16[8,64,512]{2,1,0:T(8,128)(2,1)} %copy-done.4, bf16[8,64,512]{2,1,0:T(8,128)(2,1)} %copy-done.5), custom_call_target="tpu_custom_call" | custom-call | bytes 2097152 | tf_op jit(solution)/shard_map/pick/pallas_call | solution.py:78
  45.1 2.4 %collective-permute-start.4 = (bf16[512,512]{1,0:T(8,128)(2,1)S(1)}, bf16[512,512]{1,0:T(8,128)(2,1)}, u32[]{:S(2)}, u32[]{:S(2)}) collective-permute-start(bf16[512,512]{1,0:T(8,128)(2,1)S(1)} %bitcast.5), channel_id=1, source_target_pairs={{0,8},{8,0},{1,9},{9,1},{2,10},{10,2},{3,11},{11,3},{4,12},{12,4},... | collective-permute-start | bytes 1572872 | tf_op jit(solution)/shard_map/ppermute | solution.py:39
  47.5 5.2 %all-to-all-start.1 = ((bf16[8,64,512]{2,1,0:T(8,128)(2,1)}), bf16[8,64,512]{2,1,0:T(8,128)(2,1)S(1)}, u32[]{:S(2)}, u32[]{:S(2)}) async-start(bf16[8,64,512]{2,1,0:T(8,128)(2,1)} %pick.1), calls=%async_computation.1 | async-start | bytes 1048576 | tf_op jit(solution)/shard_map/all_to_all | solution.py:163
  52.7 0.0 collective-permute-done.4.other_ref
  52.7 1.9 %collective-permute-start.5 = (bf16[512,512]{1,0:T(8,128)(2,1)S(1)}, bf16[512,512]{1,0:T(8,128)(2,1)S(1)}, u32[]{:S(2)}, u32[]{:S(2)}) collective-permute-start(bf16[512,512]{1,0:T(8,128)(2,1)S(1)} %bitcast.6), channel_id=1, source_target_pairs={{0,16},{8,24},{16,32},{24,40},{32,48},{40,56},{48,0},{56,8},{64,80... | collective-permute-start | bytes 1572872 | tf_op jit(solution)/shard_map/ppermute | solution.py:31
  54.6 4.6 %collective-permute-start.6 = (bf16[512,512]{1,0:T(8,128)(2,1)S(1)}, bf16[512,512]{1,0:T(8,128)(2,1)S(1)}, u32[]{:S(2)}, u32[]{:S(2)}) collective-permute-start(bf16[512,512]{1,0:T(8,128)(2,1)S(1)} %bitcast.7), channel_id=1, source_target_pairs={{0,48},{8,56},{16,0},{24,8},{32,16},{40,24},{48,32},{56,40},{64,11... | collective-permute-start | bytes 1572872 | tf_op jit(solution)/shard_map/ppermute | solution.py:31
  59.3 0.6 constant_dynamic-slice_fusion
  62.4 8.3 %all-to-all-done.1 = bf16[8,64,512]{2,1,0:T(8,128)(2,1)S(1)} async-done(((bf16[8,64,512]{2,1,0:T(8,128)(2,1)}), bf16[8,64,512]{2,1,0:T(8,128)(2,1)S(1)}, u32[]{:S(2)}, u32[]{:S(2)}) %all-to-all-start.1) | async-done | bytes 524320 | tf_op jit(solution)/shard_map/all_to_all | solution.py:163
  70.7 0.0 collective-permute-done.5
  70.7 0.0 collective-permute-done.6
  70.7 1.0 broadcast_select_fusion
  71.7 0.0 copy-start
  71.7 1.0 broadcast_in_dim.3
  72.7 4.4 %collective-permute-start.7 = (bf16[512,512]{1,0:T(8,128)(2,1)}, bf16[512,512]{1,0:T(8,128)(2,1)}, u32[]{:S(2)}, u32[]{:S(2)}) collective-permute-start(bf16[512,512]{1,0:T(8,128)(2,1)} %get-tuple-element.16), channel_id=1, source_target_pairs={{0,16},{16,32},{32,48},{48,0},{64,80},{80,96},{96,112},{112,64},{1... | collective-permute-start | bytes 1572872 | tf_op jit(solution)/shard_map/ppermute | solution.py:172
  77.1 1.9 %collective-permute-start.8 = (bf16[1024,512]{1,0:T(8,128)(2,1)S(1)}, bf16[1024,512]{1,0:T(8,128)(2,1)S(1)}, u32[]{:S(2)}, u32[]{:S(2)}) collective-permute-start(bf16[1024,512]{1,0:T(8,128)(2,1)S(1)} %get-tuple-element.18.mine_close_ref), channel_id=1, source_target_pairs={{0,8},{8,0},{1,9},{9,1},{2,10},{10,2},{3,11},{11,3},{4,12},{12,4},... | collective-permute-start | bytes 3145736 | tf_op jit(solution)/shard_map/ppermute | solution.py:39
  79.0 6.7 %all-to-all-start.2 = ((bf16[8,64,512]{2,1,0:T(8,128)(2,1)}), bf16[8,64,512]{2,1,0:T(8,128)(2,1)S(1)}, u32[]{:S(2)}, u32[]{:S(2)}) async-start(bf16[8,64,512]{2,1,0:T(8,128)(2,1)} %broadcast_in_dim.3), calls=%async_computation.2 | async-start | bytes 1048576 | tf_op jit(solution)/shard_map/all_to_all | solution.py:171
  85.8 0.0 collective-permute-done.7.mine_far_ref
  85.8 2.7 %collective-permute-start.9 = (bf16[512,512]{1,0:T(8,128)(2,1)}, bf16[512,512]{1,0:T(8,128)(2,1)}, u32[]{:S(2)}, u32[]{:S(2)}) collective-permute-start(bf16[512,512]{1,0:T(8,128)(2,1)} %collective-permute-done.7.mine_far_ref), channel_id=1, source_target_pairs={{0,8},{8,0},{1,9},{9,1},{2,10},{10,2},{3,11},{11,3},{4,12},{12,4},... | collective-permute-start | bytes 1572872 | tf_op jit(solution)/shard_map/ppermute | solution.py:39
  89.1 1.2 %collective-permute-done.9.other_far_ref = bf16[512,512]{1,0:T(8,128)(2,1)} collective-permute-done((bf16[512,512]{1,0:T(8,128)(2,1)}, bf16[512,512]{1,0:T(8,128)(2,1)}, u32[]{:S(2)}, u32[]{:S(2)}) %collective-permute-start.9) | collective-permute-done | bytes 524320 | tf_op jit(solution)/shard_map/ppermute | solution.py:39
  90.3 0.0 collective-permute-done.8.other_close_ref
  90.3 0.0 copy-start.3
  90.3 0.0 all-gather.2.cloned.1.call-done.rows_ref
  90.3 0.0 copy-done.1
  90.3 0.0 copy-done
  90.3 1.0 copy-done.3
  91.3 6.7 %base.1.base_ref = f32[512,512]{1,0:T(8,128)} custom-call(bf16[512,4096]{1,0:T(8,128)(2,1)} %all-gather.2.cloned.1.call-done.rows_ref, bf16[512,512]{1,0:T(8,128)(2,1)} %bitcast.8, bf16[1024,512]{1,0:T(8,128)(2,1)} %copy-done, bf16[512,512]{1,0:T(8,128)(2,1)} %collective-permute-done.7.mine_far_ref, bf16[512,512]{1,0:T(8,128)(2,1)} %collective-permute-done.4.other_ref, ...), custom_call_target="tpu_custom_call" | custom-call | flops 2147483648 | bytes 9437184 | tf_op jit(solution)/shard_map/base/pallas_call | solution.py:177
  98.0 5.7 %all-to-all-done.2.adapters = bf16[8,64,512]{2,1,0:T(8,128)(2,1)S(1)} async-done(((bf16[8,64,512]{2,1,0:T(8,128)(2,1)}), bf16[8,64,512]{2,1,0:T(8,128)(2,1)S(1)}, u32[]{:S(2)}, u32[]{:S(2)}) %all-to-all-start.2) | async-done | bytes 524320 | tf_op jit(solution)/shard_map/all_to_all | solution.py:171
  103.7 0.0 copy-start.2
  103.7 0.8 copy-done.2
  104.5 5.1 %adapt.1 = bf16[512,512]{1,0:T(8,128)(2,1)} custom-call(s32[1]{0:T(128)S(6)} %copy.13.length_ref, bf16[512,4096]{1,0:T(8,128)(2,1)} %all-gather.2.cloned.1.call-done.rows_ref, f32[512,512]{1,0:T(8,128)} %base.1.base_ref, bf16[8,64,512]{2,1,0:T(8,128)(2,1)} %copy-done.2), custom_call_target="tpu_custom_call" | custom-call | flops 134217728 | bytes 6291456 | tf_op jit(solution)/shard_map/adapt/pallas_call | solution.py:192
  (7 shorter events, 0.1 us)
Async XLA Ops:
  6.5 83.8 %all-gather.2.cloned.1.call-start = ((), (), s32[]{:S(2)}) async-start(), calls=%async_computation.3 | async-start | bytes 4718592 | tf_op jit(solution)/shard_map/all_gather | solution.py:156
  9.5 31.7 %all-to-all-start = ((bf16[8,80,512]{2,1,0:T(8,128)(2,1)}), bf16[8,80,512]{2,1,0:T(8,128)(2,1)S(1)}, u32[]{:S(2)}, u32[]{:S(2)}) async-start(bf16[8,80,512]{2,1,0:T(8,128)(2,1)} %get-tuple-element.12), calls=%async_computation | async-start | bytes 1310720 | tf_op jit(solution)/shard_map/all_to_all | solution.py:157
  20.4 10.9 %collective-permute-start = (bf16[2,64,512]{2,1,0:T(8,128)(2,1)}, bf16[2,64,512]{2,1,0:T(8,128)(2,1)S(1)}, u32[]{:S(2)}, u32[]{:S(2)}) collective-permute-start(bf16[2,64,512]{2,1,0:T(8,128)(2,1)} %get-tuple-element.13), channel_id=1, source_target_pairs={{0,16},{8,24},{16,32},{24,40},{32,48},{40,56},{48,0},{56,8},{64,80... | collective-permute-start | bytes 393224 | tf_op jit(solution)/shard_map/ppermute | solution.py:31
  23.5 7.8 %collective-permute-start.1 = (bf16[2,64,512]{2,1,0:T(8,128)(2,1)}, bf16[2,64,512]{2,1,0:T(8,128)(2,1)S(1)}, u32[]{:S(2)}, u32[]{:S(2)}) collective-permute-start(bf16[2,64,512]{2,1,0:T(8,128)(2,1)} %get-tuple-element.13), channel_id=1, source_target_pairs={{0,48},{8,56},{16,0},{24,8},{32,16},{40,24},{48,32},{56,40},{64,11... | collective-permute-start | bytes 393224 | tf_op jit(solution)/shard_map/ppermute | solution.py:31
  26.9 7.7 %collective-permute-start.2 = (bf16[2,64,512]{2,1,0:T(8,128)(2,1)}, bf16[2,64,512]{2,1,0:T(8,128)(2,1)S(1)}, u32[]{:S(2)}, u32[]{:S(2)}) collective-permute-start(bf16[2,64,512]{2,1,0:T(8,128)(2,1)} %get-tuple-element.13), channel_id=1, source_target_pairs={{0,32},{8,40},{16,48},{24,56},{32,0},{40,8},{48,16},{56,24},{64,96... | collective-permute-start | bytes 393224 | tf_op jit(solution)/shard_map/ppermute | solution.py:31
  34.7 7.4 %copy-start.4 = (bf16[8,64,512]{2,1,0:T(8,128)(2,1)}, bf16[8,64,512]{2,1,0:T(8,128)(2,1)S(1)}, u32[]{:S(2)}) copy-start(bf16[8,64,512]{2,1,0:T(8,128)(2,1)S(1)} %constant_dynamic-update-slice_fusion.mine_ref) | copy-start | bytes 1572868
  34.7 7.4 %collective-permute-start.3 = (bf16[8,64,512]{2,1,0:T(8,128)(2,1)S(1)}, bf16[8,64,512]{2,1,0:T(8,128)(2,1)S(1)}, u32[]{:S(2)}, u32[]{:S(2)}) collective-permute-start(bf16[8,64,512]{2,1,0:T(8,128)(2,1)S(1)} %constant_dynamic-update-slice_fusion.mine_ref), channel_id=1, source_target_pairs={{0,8},{8,0},{1,9},{9,1},{2,10},{10,2},{3,11},{11,3},{4,12},{12,4},... | collective-permute-start | bytes 1572872 | tf_op jit(solution)/shard_map/ppermute | solution.py:39
  41.2 49.1 %copy-start.1 = (bf16[8,64,512]{2,1,0:T(8,128)(2,1)}, bf16[8,64,512]{2,1,0:T(8,128)(2,1)S(1)}, u32[]{:S(2)}) copy-start(bf16[8,64,512]{2,1,0:T(8,128)(2,1)S(1)} %slice.8) | copy-start | bytes 1572868
  42.1 0.8 copy-start.5
  45.1 7.6 %collective-permute-start.4 = (bf16[512,512]{1,0:T(8,128)(2,1)S(1)}, bf16[512,512]{1,0:T(8,128)(2,1)}, u32[]{:S(2)}, u32[]{:S(2)}) collective-permute-start(bf16[512,512]{1,0:T(8,128)(2,1)S(1)} %bitcast.5), channel_id=1, source_target_pairs={{0,8},{8,0},{1,9},{9,1},{2,10},{10,2},{3,11},{11,3},{4,12},{12,4},... | collective-permute-start | bytes 1572872 | tf_op jit(solution)/shard_map/ppermute | solution.py:39
  47.5 23.2 %all-to-all-start.1 = ((bf16[8,64,512]{2,1,0:T(8,128)(2,1)}), bf16[8,64,512]{2,1,0:T(8,128)(2,1)S(1)}, u32[]{:S(2)}, u32[]{:S(2)}) async-start(bf16[8,64,512]{2,1,0:T(8,128)(2,1)} %pick.1), calls=%async_computation.1 | async-start | bytes 1048576 | tf_op jit(solution)/shard_map/all_to_all | solution.py:163
  52.7 18.0 %collective-permute-start.5 = (bf16[512,512]{1,0:T(8,128)(2,1)S(1)}, bf16[512,512]{1,0:T(8,128)(2,1)S(1)}, u32[]{:S(2)}, u32[]{:S(2)}) collective-permute-start(bf16[512,512]{1,0:T(8,128)(2,1)S(1)} %bitcast.6), channel_id=1, source_target_pairs={{0,16},{8,24},{16,32},{24,40},{32,48},{40,56},{48,0},{56,8},{64,80... | collective-permute-start | bytes 1572872 | tf_op jit(solution)/shard_map/ppermute | solution.py:31
  54.6 16.1 %collective-permute-start.6 = (bf16[512,512]{1,0:T(8,128)(2,1)S(1)}, bf16[512,512]{1,0:T(8,128)(2,1)S(1)}, u32[]{:S(2)}, u32[]{:S(2)}) collective-permute-start(bf16[512,512]{1,0:T(8,128)(2,1)S(1)} %bitcast.7), channel_id=1, source_target_pairs={{0,48},{8,56},{16,0},{24,8},{32,16},{40,24},{48,32},{56,40},{64,11... | collective-permute-start | bytes 1572872 | tf_op jit(solution)/shard_map/ppermute | solution.py:31
  71.7 18.6 %copy-start = (bf16[1024,512]{1,0:T(8,128)(2,1)}, bf16[1024,512]{1,0:T(8,128)(2,1)S(1)}, u32[]{:S(2)}) copy-start(bf16[1024,512]{1,0:T(8,128)(2,1)S(1)} %get-tuple-element.18.mine_close_ref) | copy-start | bytes 3145732
  72.7 13.1 %collective-permute-start.7 = (bf16[512,512]{1,0:T(8,128)(2,1)}, bf16[512,512]{1,0:T(8,128)(2,1)}, u32[]{:S(2)}, u32[]{:S(2)}) collective-permute-start(bf16[512,512]{1,0:T(8,128)(2,1)} %get-tuple-element.16), channel_id=1, source_target_pairs={{0,16},{16,32},{32,48},{48,0},{64,80},{80,96},{96,112},{112,64},{1... | collective-permute-start | bytes 1572872 | tf_op jit(solution)/shard_map/ppermute | solution.py:172
  77.1 13.2 %collective-permute-start.8 = (bf16[1024,512]{1,0:T(8,128)(2,1)S(1)}, bf16[1024,512]{1,0:T(8,128)(2,1)S(1)}, u32[]{:S(2)}, u32[]{:S(2)}) collective-permute-start(bf16[1024,512]{1,0:T(8,128)(2,1)S(1)} %get-tuple-element.18.mine_close_ref), channel_id=1, source_target_pairs={{0,8},{8,0},{1,9},{9,1},{2,10},{10,2},{3,11},{11,3},{4,12},{12,4},... | collective-permute-start | bytes 3145736 | tf_op jit(solution)/shard_map/ppermute | solution.py:39
  79.0 24.7 %all-to-all-start.2 = ((bf16[8,64,512]{2,1,0:T(8,128)(2,1)}), bf16[8,64,512]{2,1,0:T(8,128)(2,1)S(1)}, u32[]{:S(2)}, u32[]{:S(2)}) async-start(bf16[8,64,512]{2,1,0:T(8,128)(2,1)} %broadcast_in_dim.3), calls=%async_computation.2 | async-start | bytes 1048576 | tf_op jit(solution)/shard_map/all_to_all | solution.py:171
  85.8 4.6 %collective-permute-start.9 = (bf16[512,512]{1,0:T(8,128)(2,1)}, bf16[512,512]{1,0:T(8,128)(2,1)}, u32[]{:S(2)}, u32[]{:S(2)}) collective-permute-start(bf16[512,512]{1,0:T(8,128)(2,1)} %collective-permute-done.7.mine_far_ref), channel_id=1, source_target_pairs={{0,8},{8,0},{1,9},{9,1},{2,10},{10,2},{3,11},{11,3},{4,12},{12,4},... | collective-permute-start | bytes 1572872 | tf_op jit(solution)/shard_map/ppermute | solution.py:39
  90.3 1.0 copy-start.3
  103.7 0.8 copy-start.2
Sparse Core Ops, SparseCore 0:
  9.7 62.6 all-gather.1
